TPU v7x, 128 devices: a whole 4x4x4 slice. The times are simulated.
128 devices in a mesh: head: 8 (over x, z_lo), ctx: 16 (over y, z_hi, core).
Axes of the slice: x: 4, y: 4, z: 4 (z_hi: 2, z_lo: 2; z = z_hi * 2 + z_lo), core: 2. Of those that a mesh axis runs over, the one named last changes fastest.
Arguments:
- query_states: bfloat16 [8, 16, 64, 4096], P(None, 'ctx', None, 'head'), may hold values from -8 to 8
- key_states: bfloat16 [8, 16, 64, 1024], P(None, 'ctx', None, 'head'), may hold values from -4 to 4
- value_states: bfloat16 [8, 16, 64, 1024], P(None, 'ctx', None, 'head'), may hold values from -6 to 6
- out_grad: bfloat16 [8, 16, 64, 4096], P(None, 'ctx', None, 'head'), may hold values from -6 to 6
- out_weight: bfloat16 [4096, 4096], P('head'), may hold values from -0.125 to 0.125
- vertical_blocks: int32 [8, 8, 16, 32], P('head', None, 'ctx'), may hold values from 0 to 127, as said below
- slash_offsets: int32 [8, 8, 16, 8], P('head', None, 'ctx'), may hold values from 0 to 15, as said below
Outputs:
- layer_out: bfloat16 [8, 16, 64, 4096], P(None, 'ctx', None, 'head')
- query_grad: bfloat16 [8, 16, 64, 4096], P(None, 'ctx', None, 'head')
- key_grad: bfloat16 [8, 16, 64, 1024], P(None, 'ctx', None, 'head')
- value_grad: bfloat16 [8, 16, 64, 1024], P(None, 'ctx', None, 'head')
Inputs may be any that keep to these rules, and one draw needn't show every extreme that they name: `vertical_blocks`: entries of one vertical list are distinct; a kept vertical block never equals a kept slash block of the same list. `slash_offsets`: the first offset of every list is 0; the offsets of one list are distinct.
All inputs are finite; a program needn't handle non-finite values.
Results may differ from a plain program's by a relative error of at most 0.023.
Values may be sent and summed in bfloat16 or wider, within the bound.
A program may use at most 192 MiB of HBM per device.

v0:
```python
import math

import jax
import jax.numpy as jnp
from jax import lax
from jax.sharding import PartitionSpec as P

HQ = 32
KVH = 8
HD = 128
NV = 32
NS = 8


def from_behind(value, axis, steps):
    count = lax.axis_size(axis)
    pairs = [(source, (source + steps) % count) for source in range(count)]
    return lax.ppermute(value, axis, pairs)


def entry_table(block_ids, vertical, slash_rows, nblk, block_rows):
    raw_index = jnp.concatenate([vertical, block_ids[:, None] - slash_rows], axis=1)
    is_kept = (raw_index >= 0) & (raw_index <= block_ids[:, None])
    on_diagonal = raw_index == block_ids[:, None]
    query_pos = lax.broadcasted_iota(jnp.int32, (block_rows, block_rows), 0)
    key_pos = lax.broadcasted_iota(jnp.int32, (block_rows, block_rows), 1)
    lower_tri = key_pos <= query_pos
    allowed = is_kept[:, None, :, None] & (
        jnp.logical_not(on_diagonal)[:, None, :, None] | lower_tri[None, :, None, :]
    )
    return (jnp.clip(raw_index, 0, nblk - 1), allowed)


def attend_group(query_rows, key_rows, value_rows, grad_rows, allowed, score_scale):
    scores = (
        jnp.einsum("rqhd,rekd->rqhek", query_rows, key_rows, preferred_element_type=jnp.float32)
        * score_scale
    )
    scores = jnp.where(allowed[:, :, None], scores, -jnp.inf)
    row_max = jnp.max(scores, axis=(3, 4), keepdims=True)
    expo = jnp.exp(scores - row_max)
    row_total = jnp.sum(expo, axis=(3, 4), keepdims=True)
    log_norm = row_max + jnp.log(row_total)
    probs = (expo / row_total).astype(jnp.bfloat16)
    attended = jnp.einsum(
        "rqhek,rekd->rqhd", probs, value_rows, preferred_element_type=jnp.float32
    ).astype(jnp.bfloat16)
    probs_back = jnp.exp(scores - log_norm)
    grad_probs = jnp.einsum(
        "rqhd,rekd->rqhek", grad_rows, value_rows, preferred_element_type=jnp.float32
    )
    row_delta = jnp.sum(grad_rows.astype(jnp.float32) * attended.astype(jnp.float32), axis=-1)[
        :, :, :, None, None
    ]
    grad_scores = (probs_back * (grad_probs - row_delta)).astype(jnp.bfloat16)
    probs_low = probs_back.astype(jnp.bfloat16)
    value_part = jnp.einsum(
        "rqhek,rqhd->rekd", probs_low, grad_rows, preferred_element_type=jnp.float32
    )
    key_part = (
        jnp.einsum("rqhek,rqhd->rekd", grad_scores, query_rows, preferred_element_type=jnp.float32)
        * score_scale
    )
    query_part = (
        jnp.einsum("rqhek,rekd->rqhd", grad_scores, key_rows, preferred_element_type=jnp.float32)
        * score_scale
    ).astype(jnp.bfloat16)
    return (attended, query_part, key_part, value_part)


def on_device(
    query_states, key_states, value_states, out_grad, out_weight, vertical_blocks, slash_offsets
):
    local_blocks = query_states.shape[0]
    block_rows = query_states.shape[2]
    kv_local = key_states.shape[3] // HD
    heads_per_kv = HQ // KVH
    n_ctx = lax.axis_size("ctx")
    nblk = local_blocks * n_ctx
    my_index = lax.axis_index("ctx")
    model_width = out_weight.shape[1]
    tok_rows = local_blocks * block_rows
    score_scale = 1.0 / math.sqrt(HD)
    shard_piece = lax.all_gather(out_grad, "head", axis=3, tiled=True)
    row_count = shard_piece.shape[3]
    flat_rows = shard_piece.reshape(tok_rows, row_count)
    attn_grad = jnp.einsum(
        "tn,wn->tw", flat_rows, out_weight, preferred_element_type=jnp.float32
    ).astype(jnp.bfloat16)
    keys_all, values_all = (
        lax.all_gather(key_states, "ctx", axis=1, tiled=True),
        lax.all_gather(value_states, "ctx", axis=1, tiled=True),
    )
    keys_all = keys_all.reshape(nblk, block_rows, kv_local, HD)
    values_all = values_all.reshape(nblk, block_rows, kv_local, HD)
    per_step = math.gcd(local_blocks, 8)
    step_count = local_blocks // per_step
    block_ids = (jnp.arange(local_blocks, dtype=jnp.int32) * n_ctx + my_index).reshape(
        step_count, per_step
    )
    q_all = query_states.reshape(step_count, per_step, block_rows, kv_local * heads_per_kv, HD)
    g_all = attn_grad.reshape(step_count, per_step, block_rows, kv_local * heads_per_kv, HD)
    vertical_all = vertical_blocks.reshape(kv_local, step_count, per_step, NV)
    slash_all = slash_offsets.reshape(kv_local, step_count, per_step, NS)
    key_table = keys_all[:, :, 0]
    value_table = values_all[:, :, 0]

    def step_fn(running, inputs, key_table=key_table, value_table=value_table):
        q_rows, g_rows, ids_now, vertical, slash_rows = inputs
        key_index, allowed = entry_table(ids_now, vertical, slash_rows, nblk, block_rows)
        attended, query_part, key_part, value_part = attend_group(
            q_rows, key_table[key_index], value_table[key_index], g_rows, allowed, score_scale
        )
        update = jnp.stack([key_part, value_part], axis=3).reshape(-1, block_rows, 2, HD)
        running = running.at[key_index.reshape(-1)].add(update)
        return (running, (attended, query_part))

    initial = jnp.zeros((nblk, block_rows, 2, HD), jnp.float32)
    partial_value, (attended_rows, query_rows) = lax.scan(
        step_fn, initial, (q_all, g_all, block_ids, vertical_all[0], slash_all[0])
    )
    attended_list = attended_rows.reshape(tok_rows, heads_per_kv * HD)
    query_list = query_rows.reshape(tok_rows, heads_per_kv * HD)
    partial_list = [partial_value]
    layer_terms = jnp.dot(attended_list, out_weight, preferred_element_type=jnp.float32).reshape(
        local_blocks, 1, block_rows, model_width
    )
    layer_out = lax.psum_scatter(
        layer_terms.astype(jnp.bfloat16), "head", scatter_dimension=3, tiled=True
    )
    query_grad = query_list.reshape(query_states.shape)
    stacked = jnp.stack(partial_list, axis=3)
    owner_term = (
        stacked.reshape(local_blocks, n_ctx, block_rows, 2 * kv_local * HD)
        .transpose(1, 0, 2, 3)
        .reshape(n_ctx * tok_rows, 2 * kv_local * HD)
    )

    def owner_rows(owner):
        return lax.dynamic_slice_in_dim(owner_term, owner * tok_rows, tok_rows, 0)

    def pass_step(turn, carried):
        arrived = from_behind(carried.astype(jnp.bfloat16), "ctx", 1).astype(carried.dtype)
        return arrived + owner_rows((my_index + n_ctx - 1 - turn) % n_ctx)

    summed_grad = lax.fori_loop(1, n_ctx, pass_step, owner_rows((my_index + n_ctx - 1) % n_ctx))
    kv_grad = summed_grad.reshape(local_blocks, 1, block_rows, 2, kv_local * HD)
    key_grad = kv_grad[:, :, :, 0].astype(jnp.bfloat16)
    value_grad = kv_grad[:, :, :, 1].astype(jnp.bfloat16)
    return (layer_out, query_grad, key_grad, value_grad)


def solution(mesh):
    return jax.shard_map(
        on_device,
        mesh=mesh,
        in_specs=(
            P(None, "ctx", None, "head"),
            P(None, "ctx", None, "head"),
            P(None, "ctx", None, "head"),
            P(None, "ctx", None, "head"),
            P("head", None),
            P("head", None, "ctx", None),
            P("head", None, "ctx", None),
        ),
        out_specs=(
            P(None, "ctx", None, "head"),
            P(None, "ctx", None, "head"),
            P(None, "ctx", None, "head"),
            P(None, "ctx", None, "head"),
        ),
        check_vma=False,
    )
```

profile of v0, /device:TPU:2, one launch (start us, length us, event | category | flops | bytes accessed | tf_op | source)
XLA Modules:
  0.0 601.5 jit_solution(14166530016190835103)
XLA Ops:
  7.2 0.7 all-gather.6.cloned.1.call-update
  7.9 0.7 all-gather.4.cloned.1.call-update
  9.5 0.8 fusion.34
  10.2 0.8 compare_select_fusion
  11.1 1.2 squeeze.23
  12.2 0.8 broadcast_subtract_fusion
  13.0 0.8 broadcast_clamp_fusion
  14.5 0.8 compare_and_fusion
  15.3 1.8 or_and_fusion
  17.1 44.2 %all-gather.6.cloned.1.call-done = bf16[8,16,64,128]{3,2,1,0:T(8,128)(2,1)} async-done(((bf16[8,1,64,128]{3,2,1,0:T(8,128)(2,1)}), bf16[8,16,64,128]{3,2,1,0:T(8,128)(2,1)}) %all-gather.6.cloned.1.call-update) | async-done | bytes 2097168 | tf_op jit(solution)/shard_map/all_gather | solution.py:92
  61.3 5.2 gather_fusion.1
  66.5 44.4 %all-gather.4.cloned.1.call-done = bf16[8,16,64,128]{3,2,1,0:T(8,128)(2,1)} async-done(((bf16[8,1,64,128]{3,2,1,0:T(8,128)(2,1)}), bf16[8,16,64,128]{3,2,1,0:T(8,128)(2,1)}) %all-gather.4.cloned.1.call-update) | async-done | bytes 2097168 | tf_op jit(solution)/shard_map/all_gather | solution.py:91
  110.9 5.3 gather_fusion
  116.2 19.5 %fusion.2 = (f32[8,64,4]{1,2,0:T(4,128)S(1)}, f32[8,40,64,64,4]{3,2,4,1,0:T(8,128)}) fusion(pred[8,64,40,64]{1,3,2,0:T(8,128)(4,1)S(1)} %or_and_fusion, bf16[8,40,64,128,1]{3,2,4,1,0:T(8,128)(2,1)} %bitcast.118, bf16[8,64,4,128,1]{3,2,1,0,4:T(4,128)(2,1)S(1)} %bitcast.129), kind=kOutput, calls=%fused_computation.11 | convolution fusion | flops 1357903872 | bytes 28057600 | tf_op jit(solution)/shard_map/while/body/eval_jaxpr/rqhd,rekd->rqhek/dot_general | solution.py:36
  135.7 19.0 %fusion = f32[8,64,4]{1,2,0:T(4,128)S(1)} fusion(f32[8,40,64,64,4]{3,2,4,1,0:T(8,128)} %get-tuple-element.178, f32[8,64,4]{1,2,0:T(4,128)S(1)} %get-tuple-element.177, pred[8,64,40,64]{1,3,2,0:T(8,128)(4,1)S(1)} %or_and_fusion), kind=kLoop, calls=%fused_computation.9 | loop fusion | flops 20969472 | bytes 22298624 | tf_op jit(solution)/shard_map/while/body/eval_jaxpr/reduce_sum | solution.py:42
  154.7 46.3 %all-gather.8.cloned.1.call-done = bf16[8,1,64,4096]{3,2,1,0:T(8,128)(2,1)} async-done(((bf16[8,1,64,512]{3,2,1,0:T(8,128)(2,1)}), bf16[8,1,64,4096]{3,2,1,0:T(8,128)(2,1)}) %all-gather.8.cloned.1.call-update) | async-done | bytes 4194320 | tf_op jit(solution)/shard_map/all_gather | solution.py:84
  201.0 6.6 %convolution_convert_fusion.1 = bf16[512,512]{1,0:T(8,128)(2,1)} fusion(bf16[512,4096]{1,0:T(8,128)(2,1)} %bitcast.142, bf16[512,4096]{1,0:T(8,128)(2,1)} %param.13), kind=kOutput, calls=%fused_computation.25 | convolution fusion | flops 2147745792 | bytes 8912896 | tf_op jit(solution)/shard_map/tn,wn->tw/dot_general | solution.py:87
  207.6 1.2 squeeze.24
  208.8 20.4 %multiply_reduce_fusion = (f32[8,64,4]{1,2,0:T(4,128)S(1)}, bf16[8,64,4,128]{3,1,2,0:T(8,128)(2,1)}) fusion(bf16[8,64,4,128]{3,2,1,0:T(4,128)(2,1)S(1)} %squeeze.24, bf16[8,40,64,128,1]{3,2,4,1,0:T(8,128)(2,1)} %bitcast.126, f32[8,40,64,64,4]{3,2,4,1,0:T(8,128)} %get-tuple-element.178, f32[8,64,4]{1,2,0:T(4,128)S(1)} %fusion, ...), kind=kOutput, calls=%fused_computation.27 | convolution fusion | flops 1369700352 | bytes 28598272 | tf_op jit(solution)/shard_map/while/body/eval_jaxpr/rqhek,rekd->rqhd/dot_general | solution.py:45
  229.2 6.7 %fusion.7 = bf16[8,1,64,4096]{3,2,0,1:T(8,128)(2,1)} fusion(bf16[512,4096]{1,0:T(8,128)(2,1)} %param.13, bf16[8,64,4,128]{3,1,2,0:T(8,128)(2,1)} %get-tuple-element.180), kind=kOutput, calls=%fused_computation.19 | convolution fusion | flops 2149580800 | bytes 8912896 | tf_op jit(solution)/shard_map/dot_general | solution.py:125
  235.9 26.1 %multiply_convert_fusion = bf16[8,64,4,40,64]{1,4,2,3,0:T(8,128)(2,1)} fusion(f32[8,40,64,64,4]{3,2,4,1,0:T(8,128)} %get-tuple-element.178, f32[8,64,4]{1,2,0:T(4,128)S(1)} %get-tuple-element.179, f32[8,64,4]{1,2,0:T(4,128)S(1)} %bitcast.138, pred[8,64,40,64]{1,3,2,0:T(8,128)(4,1)S(1)} %or_and_fusion, bf16[8,40,64,128,1]{3,2,4,1,0:T(8,128)(2,1)} %bitcast.127, ...), kind=kOutput, calls=%fused_computation.5 | convolution fusion | flops 1373634560 | bytes 38551552 | tf_op jit(solution)/shard_map/while/body/eval_jaxpr/rqhd,rekd->rqhek/dot_general | solution.py:49
  262.0 11.7 %fusion.11 = bf16[8,64,4,128]{3,1,2,0:T(8,128)(2,1)S(1)} fusion(bf16[8,64,4,40,64]{1,4,2,3,0:T(8,128)(2,1)} %multiply_convert_fusion, bf16[8,40,64,128,1]{3,2,4,1,0:T(8,128)(2,1)} %bitcast.119), kind=kOutput, calls=%fused_computation.24 | convolution fusion | flops 1342701568 | bytes 16252928 | tf_op jit(solution)/shard_map/while/body/eval_jaxpr/rqhek,rekd->rqhd/dot_general | solution.py:65
  274.1 1.0 reshape_reshape.3
  275.1 15.4 %bitcast_multiply_fusion = f32[8,40,64,128]{3,2,1,0:T(8,128)} fusion(bf16[8,64,4,40,64]{1,4,2,3,0:T(8,128)(2,1)} %multiply_convert_fusion, bf16[8,64,4,128,1]{3,2,1,0,4:T(4,128)(2,1)} %bitcast.130), kind=kOutput, calls=%fused_computation.16 | convolution fusion | flops 1344798720 | bytes 21495808 | tf_op jit(solution)/shard_map/while/body/eval_jaxpr/rqhek,rqhd->rekd/dot_general | solution.py:61
  290.6 22.5 %fusion.3 = f32[8,40,64,128,1]{3,2,4,1,0:T(8,128)} fusion(f32[8,40,64,64,4]{3,2,4,1,0:T(8,128)} %get-tuple-element.178, f32[8,64,4]{1,2,0:T(4,128)S(1)} %bitcast.139, pred[8,64,40,64]{1,3,2,0:T(8,128)(4,1)S(1)} %or_and_fusion, bf16[8,64,4,128,1]{3,2,1,0,4:T(4,128)(2,1)S(1)} %bitcast.132), kind=kOutput, calls=%fused_computation.13 | convolution fusion | flops 1363148800 | bytes 33300480 | tf_op jit(solution)/shard_map/while/body/eval_jaxpr/rqhek,rqhd->rekd/dot_general | solution.py:57
  313.1 16.5 %pad_maximum_fusion = f32[320,64,2,128]{3,1,2,0:T(8,128)} fusion(f32[320,64,1,128]{3,1,2,0:T(8,128)} %bitcast.125, f32[320,64,1,128]{3,1,2,0:T(8,128)} %bitcast.124), kind=kLoop, calls=%fused_computation.12 | loop fusion | flops 5242880 | bytes 41943040 | tf_op jit(solution)/shard_map/while/body/eval_jaxpr/stack | solution.py:114
  329.6 4.3 broadcast_in_dim.49
  333.9 66.6 %scatter_fusion = f32[128,64,2,128]{3,1,2,0:T(8,128)} fusion(f32[128,64,2,128]{3,1,2,0:T(8,128)} %broadcast_in_dim.49, s32[320]{0:T(512)S(1)} %copy-done.4, f32[320,64,2,128]{3,1,2,0:T(8,128)} %pad_maximum_fusion), kind=kCustom, calls=%fused_computation.2 | custom fusion | flops 5242880 | bytes 62915840 | tf_op jit(solution)/shard_map/while/body/eval_jaxpr/scatter-add | solution.py:115
  400.6 15.3 %copy.48 = f32[128,64,2,128]{3,2,1,0:T(2,128)} copy(f32[128,64,2,128]{3,1,2,0:T(8,128)} %scatter_fusion) | data formatting | bytes 16777216 | tf_op jit(solution)/shard_map/while/body/eval_jaxpr/scatter-add | solution.py:115
  415.9 11.5 %reshape_stack.3 = f32[8,16,64,256]{3,2,1,0:T(8,128)} reshape(f32[128,64,2,128]{3,2,1,0:T(2,128)} %copy.48) | data formatting | bytes 16777216 | tf_op jit(solution)/shard_map/reshape;stack | solution.py:134
  427.4 4.0 copy.49
  431.5 3.2 copy-done
  434.6 158.8 %while.10 = (s32[]{:T(128)}, bf16[512,256]{1,0:T(8,128)(2,1)S(1)}, s32[]{:T(128)}, f32[8192,256]{1,0:T(8,128)}, s32[]{:T(128)}, /*index=5*/s32[]{:T(128)}, s32[]{:T(128)}, s32[]{:T(128)}, s32[]{:T(128)}, s32[]{:T(128)}) while((s32[]{:T(128)}, bf16[512,256]{1,0:T(8,128)(2,1)S(1)}, s32[]{:T(128)}, f32[8192,256]{1,0:T(8,128)}, s32[]{:T(128)}, ...), condition=%wide.region_6.7_spmd, body=%wide.region_5.6_spmd.sunk | while | flops 393234 | bytes 2097464 | solution.py:146
  434.6 9.4 %collective-permute-done = bf16[512,256]{1,0:T(8,128)(2,1)S(1)} collective-permute-done((bf16[512,256]{1,0:T(8,128)(2,1)S(1)}, bf16[512,256]{1,0:T(8,128)(2,1)S(1)}, u32[]{:S(2)}, u32[]{:S(2)}) %collective-permute-start) | collective-permute-done | bytes 262176 | tf_op jit(solution)/shard_map/while/body/eval_jaxpr/ppermute | solution.py:18
  444.0 1.1 dynamic-slice_add_fusion.2
  445.3 9.4 %collective-permute-done = bf16[512,256]{1,0:T(8,128)(2,1)S(1)} collective-permute-done((bf16[512,256]{1,0:T(8,128)(2,1)S(1)}, bf16[512,256]{1,0:T(8,128)(2,1)S(1)}, u32[]{:S(2)}, u32[]{:S(2)}) %collective-permute-start) | collective-permute-done | bytes 262176 | tf_op jit(solution)/shard_map/while/body/eval_jaxpr/ppermute | solution.py:18
  454.6 1.1 dynamic-slice_add_fusion.2
  455.9 9.4 %collective-permute-done = bf16[512,256]{1,0:T(8,128)(2,1)S(1)} collective-permute-done((bf16[512,256]{1,0:T(8,128)(2,1)S(1)}, bf16[512,256]{1,0:T(8,128)(2,1)S(1)}, u32[]{:S(2)}, u32[]{:S(2)}) %collective-permute-start) | collective-permute-done | bytes 262176 | tf_op jit(solution)/shard_map/while/body/eval_jaxpr/ppermute | solution.py:18
  465.2 1.1 dynamic-slice_add_fusion.2
  466.4 9.4 %collective-permute-done = bf16[512,256]{1,0:T(8,128)(2,1)S(1)} collective-permute-done((bf16[512,256]{1,0:T(8,128)(2,1)S(1)}, bf16[512,256]{1,0:T(8,128)(2,1)S(1)}, u32[]{:S(2)}, u32[]{:S(2)}) %collective-permute-start) | collective-permute-done | bytes 262176 | tf_op jit(solution)/shard_map/while/body/eval_jaxpr/ppermute | solution.py:18
  475.8 1.1 dynamic-slice_add_fusion.2
  477.0 9.4 %collective-permute-done = bf16[512,256]{1,0:T(8,128)(2,1)S(1)} collective-permute-done((bf16[512,256]{1,0:T(8,128)(2,1)S(1)}, bf16[512,256]{1,0:T(8,128)(2,1)S(1)}, u32[]{:S(2)}, u32[]{:S(2)}) %collective-permute-start) | collective-permute-done | bytes 262176 | tf_op jit(solution)/shard_map/while/body/eval_jaxpr/ppermute | solution.py:18
  486.4 1.1 dynamic-slice_add_fusion.2
  487.6 9.4 %collective-permute-done = bf16[512,256]{1,0:T(8,128)(2,1)S(1)} collective-permute-done((bf16[512,256]{1,0:T(8,128)(2,1)S(1)}, bf16[512,256]{1,0:T(8,128)(2,1)S(1)}, u32[]{:S(2)}, u32[]{:S(2)}) %collective-permute-start) | collective-permute-done | bytes 262176 | tf_op jit(solution)/shard_map/while/body/eval_jaxpr/ppermute | solution.py:18
  497.0 1.1 dynamic-slice_add_fusion.2
  498.2 9.4 %collective-permute-done = bf16[512,256]{1,0:T(8,128)(2,1)S(1)} collective-permute-done((bf16[512,256]{1,0:T(8,128)(2,1)S(1)}, bf16[512,256]{1,0:T(8,128)(2,1)S(1)}, u32[]{:S(2)}, u32[]{:S(2)}) %collective-permute-start) | collective-permute-done | bytes 262176 | tf_op jit(solution)/shard_map/while/body/eval_jaxpr/ppermute | solution.py:18
  507.6 1.1 dynamic-slice_add_fusion.2
  508.8 9.4 %collective-permute-done = bf16[512,256]{1,0:T(8,128)(2,1)S(1)} collective-permute-done((bf16[512,256]{1,0:T(8,128)(2,1)S(1)}, bf16[512,256]{1,0:T(8,128)(2,1)S(1)}, u32[]{:S(2)}, u32[]{:S(2)}) %collective-permute-start) | collective-permute-done | bytes 262176 | tf_op jit(solution)/shard_map/while/body/eval_jaxpr/ppermute | solution.py:18
  518.2 1.1 dynamic-slice_add_fusion.2
  519.4 9.4 %collective-permute-done = bf16[512,256]{1,0:T(8,128)(2,1)S(1)} collective-permute-done((bf16[512,256]{1,0:T(8,128)(2,1)S(1)}, bf16[512,256]{1,0:T(8,128)(2,1)S(1)}, u32[]{:S(2)}, u32[]{:S(2)}) %collective-permute-start) | collective-permute-done | bytes 262176 | tf_op jit(solution)/shard_map/while/body/eval_jaxpr/ppermute | solution.py:18
  528.8 1.1 dynamic-slice_add_fusion.2
  530.0 9.4 %collective-permute-done = bf16[512,256]{1,0:T(8,128)(2,1)S(1)} collective-permute-done((bf16[512,256]{1,0:T(8,128)(2,1)S(1)}, bf16[512,256]{1,0:T(8,128)(2,1)S(1)}, u32[]{:S(2)}, u32[]{:S(2)}) %collective-permute-start) | collective-permute-done | bytes 262176 | tf_op jit(solution)/shard_map/while/body/eval_jaxpr/ppermute | solution.py:18
  539.4 1.1 dynamic-slice_add_fusion.2
  540.6 9.4 %collective-permute-done = bf16[512,256]{1,0:T(8,128)(2,1)S(1)} collective-permute-done((bf16[512,256]{1,0:T(8,128)(2,1)S(1)}, bf16[512,256]{1,0:T(8,128)(2,1)S(1)}, u32[]{:S(2)}, u32[]{:S(2)}) %collective-permute-start) | collective-permute-done | bytes 262176 | tf_op jit(solution)/shard_map/while/body/eval_jaxpr/ppermute | solution.py:18
  549.9 1.1 dynamic-slice_add_fusion.2
  551.2 9.4 %collective-permute-done = bf16[512,256]{1,0:T(8,128)(2,1)S(1)} collective-permute-done((bf16[512,256]{1,0:T(8,128)(2,1)S(1)}, bf16[512,256]{1,0:T(8,128)(2,1)S(1)}, u32[]{:S(2)}, u32[]{:S(2)}) %collective-permute-start) | collective-permute-done | bytes 262176 | tf_op jit(solution)/shard_map/while/body/eval_jaxpr/ppermute | solution.py:18
  560.5 1.1 dynamic-slice_add_fusion.2
  561.8 9.4 %collective-permute-done = bf16[512,256]{1,0:T(8,128)(2,1)S(1)} collective-permute-done((bf16[512,256]{1,0:T(8,128)(2,1)S(1)}, bf16[512,256]{1,0:T(8,128)(2,1)S(1)}, u32[]{:S(2)}, u32[]{:S(2)}) %collective-permute-start) | collective-permute-done | bytes 262176 | tf_op jit(solution)/shard_map/while/body/eval_jaxpr/ppermute | solution.py:18
  571.1 1.1 dynamic-slice_add_fusion.2
  572.3 9.4 %collective-permute-done = bf16[512,256]{1,0:T(8,128)(2,1)S(1)} collective-permute-done((bf16[512,256]{1,0:T(8,128)(2,1)S(1)}, bf16[512,256]{1,0:T(8,128)(2,1)S(1)}, u32[]{:S(2)}, u32[]{:S(2)}) %collective-permute-start) | collective-permute-done | bytes 262176 | tf_op jit(solution)/shard_map/while/body/eval_jaxpr/ppermute | solution.py:18
  581.7 1.1 dynamic-slice_add_fusion.2
  582.9 9.4 %collective-permute-done = bf16[512,256]{1,0:T(8,128)(2,1)S(1)} collective-permute-done((bf16[512,256]{1,0:T(8,128)(2,1)S(1)}, bf16[512,256]{1,0:T(8,128)(2,1)S(1)}, u32[]{:S(2)}, u32[]{:S(2)}) %collective-permute-start) | collective-permute-done | bytes 262176 | tf_op jit(solution)/shard_map/while/body/eval_jaxpr/ppermute | solution.py:18
  592.3 1.1 dynamic-slice_add_fusion.2
  594.0 0.7 copy_bitcast_fusion
  (42 shorter events, 3.7 us)
Async XLA Ops:
  7.2 54.1 %all-gather.6.cloned.1.call-start = ((), (), s32[]{:S(2)}) async-start(), calls=%async_computation.2 | async-start | bytes 2228224 | tf_op jit(solution)/shard_map/all_gather | solution.py:92
  7.9 103.0 %all-gather.4.cloned.1.call-start = ((), (), s32[]{:S(2)}) async-start(), calls=%async_computation.1 | async-start | bytes 2228224 | tf_op jit(solution)/shard_map/all_gather | solution.py:91
  8.6 192.4 %all-gather.8.cloned.1.call-start = ((), (), s32[]{:S(2)}) async-start(), calls=%async_computation.4 | async-start | bytes 4718592 | tf_op jit(solution)/shard_map/all_gather | solution.py:84
  9.4 585.3 %reduce-scatter.2.cloned.1.call-start = ((), (), s32[]{:S(2)}) async-start(), calls=%async_computation.3 | async-start | bytes 4718592 | tf_op jit(solution)/shard_map/reduce_scatter | solution.py:128
  12.2 104.0 %copy-start.1 = (bf16[8,64,4,128]{3,2,1,0:T(4,128)(2,1)}, bf16[8,64,4,128]{3,2,1,0:T(4,128)(2,1)S(1)}, u32[]{:S(2)}) copy-start(bf16[8,64,4,128]{3,2,1,0:T(4,128)(2,1)S(1)} %squeeze.23) | copy-start | bytes 1572868
  208.8 27.1 %copy-start.2 = (bf16[8,64,4,128]{3,2,1,0:T(4,128)(2,1)}, bf16[8,64,4,128]{3,2,1,0:T(4,128)(2,1)S(1)}, u32[]{:S(2)}) copy-start(bf16[8,64,4,128]{3,2,1,0:T(4,128)(2,1)S(1)} %squeeze.24) | copy-start | bytes 1572868
  275.1 15.4 %copy-start.3 = (bf16[8,64,4,128]{3,2,1,0:T(4,128)(2,1)S(1)}, bf16[8,64,4,128]{3,2,1,0:T(4,128)(2,1)}, u32[]{:S(2)}) copy-start(bf16[8,64,4,128]{3,2,1,0:T(4,128)(2,1)} %copy-done.2) | copy-start | bytes 1572868
  313.1 20.9 %copy-start.4 = (s32[320]{0:T(512)S(1)}, s32[320]{0:T(512)}, u32[]{:S(2)}) copy-start(s32[320]{0:T(512)} %fusion.20) | copy-start | bytes 3844
  431.4 3.2 copy-start
  434.6 9.4 %collective-permute-start = (bf16[512,256]{1,0:T(8,128)(2,1)S(1)}, bf16[512,256]{1,0:T(8,128)(2,1)S(1)}, u32[]{:S(2)}, u32[]{:S(2)}) collective-permute-start(bf16[512,256]{1,0:T(8,128)(2,1)S(1)} %get-tuple-element.219), channel_id=1, source_target_pairs={{0,1},{1,2},{2,3},{3,4},{4,5},{5,6},{6,7},{7,8},{8,9},{9,10},{10,1... | collective-permute-start | bytes 786440 | tf_op jit(solution)/shard_map/while/body/eval_jaxpr/ppermute | solution.py:18
  445.2 9.5 %collective-permute-start = (bf16[512,256]{1,0:T(8,128)(2,1)S(1)}, bf16[512,256]{1,0:T(8,128)(2,1)S(1)}, u32[]{:S(2)}, u32[]{:S(2)}) collective-permute-start(bf16[512,256]{1,0:T(8,128)(2,1)S(1)} %get-tuple-element.219), channel_id=1, source_target_pairs={{0,1},{1,2},{2,3},{3,4},{4,5},{5,6},{6,7},{7,8},{8,9},{9,10},{10,1... | collective-permute-start | bytes 786440 | tf_op jit(solution)/shard_map/while/body/eval_jaxpr/ppermute | solution.py:18
  455.7 9.5 %collective-permute-start = (bf16[512,256]{1,0:T(8,128)(2,1)S(1)}, bf16[512,256]{1,0:T(8,128)(2,1)S(1)}, u32[]{:S(2)}, u32[]{:S(2)}) collective-permute-start(bf16[512,256]{1,0:T(8,128)(2,1)S(1)} %get-tuple-element.219), channel_id=1, source_target_pairs={{0,1},{1,2},{2,3},{3,4},{4,5},{5,6},{6,7},{7,8},{8,9},{9,10},{10,1... | collective-permute-start | bytes 786440 | tf_op jit(solution)/shard_map/while/body/eval_jaxpr/ppermute | solution.py:18
  466.3 9.5 %collective-permute-start = (bf16[512,256]{1,0:T(8,128)(2,1)S(1)}, bf16[512,256]{1,0:T(8,128)(2,1)S(1)}, u32[]{:S(2)}, u32[]{:S(2)}) collective-permute-start(bf16[512,256]{1,0:T(8,128)(2,1)S(1)} %get-tuple-element.219), channel_id=1, source_target_pairs={{0,1},{1,2},{2,3},{3,4},{4,5},{5,6},{6,7},{7,8},{8,9},{9,10},{10,1... | collective-permute-start | bytes 786440 | tf_op jit(solution)/shard_map/while/body/eval_jaxpr/ppermute | solution.py:18
  476.9 9.5 %collective-permute-start = (bf16[512,256]{1,0:T(8,128)(2,1)S(1)}, bf16[512,256]{1,0:T(8,128)(2,1)S(1)}, u32[]{:S(2)}, u32[]{:S(2)}) collective-permute-start(bf16[512,256]{1,0:T(8,128)(2,1)S(1)} %get-tuple-element.219), channel_id=1, source_target_pairs={{0,1},{1,2},{2,3},{3,4},{4,5},{5,6},{6,7},{7,8},{8,9},{9,10},{10,1... | collective-permute-start | bytes 786440 | tf_op jit(solution)/shard_map/while/body/eval_jaxpr/ppermute | solution.py:18
  487.5 9.5 %collective-permute-start = (bf16[512,256]{1,0:T(8,128)(2,1)S(1)}, bf16[512,256]{1,0:T(8,128)(2,1)S(1)}, u32[]{:S(2)}, u32[]{:S(2)}) collective-permute-start(bf16[512,256]{1,0:T(8,128)(2,1)S(1)} %get-tuple-element.219), channel_id=1, source_target_pairs={{0,1},{1,2},{2,3},{3,4},{4,5},{5,6},{6,7},{7,8},{8,9},{9,10},{10,1... | collective-permute-start | bytes 786440 | tf_op jit(solution)/shard_map/while/body/eval_jaxpr/ppermute | solution.py:18
  498.1 9.5 %collective-permute-start = (bf16[512,256]{1,0:T(8,128)(2,1)S(1)}, bf16[512,256]{1,0:T(8,128)(2,1)S(1)}, u32[]{:S(2)}, u32[]{:S(2)}) collective-permute-start(bf16[512,256]{1,0:T(8,128)(2,1)S(1)} %get-tuple-element.219), channel_id=1, source_target_pairs={{0,1},{1,2},{2,3},{3,4},{4,5},{5,6},{6,7},{7,8},{8,9},{9,10},{10,1... | collective-permute-start | bytes 786440 | tf_op jit(solution)/shard_map/while/body/eval_jaxpr/ppermute | solution.py:18
  508.7 9.5 %collective-permute-start = (bf16[512,256]{1,0:T(8,128)(2,1)S(1)}, bf16[512,256]{1,0:T(8,128)(2,1)S(1)}, u32[]{:S(2)}, u32[]{:S(2)}) collective-permute-start(bf16[512,256]{1,0:T(8,128)(2,1)S(1)} %get-tuple-element.219), channel_id=1, source_target_pairs={{0,1},{1,2},{2,3},{3,4},{4,5},{5,6},{6,7},{7,8},{8,9},{9,10},{10,1... | collective-permute-start | bytes 786440 | tf_op jit(solution)/shard_map/while/body/eval_jaxpr/ppermute | solution.py:18
  519.3 9.5 %collective-permute-start = (bf16[512,256]{1,0:T(8,128)(2,1)S(1)}, bf16[512,256]{1,0:T(8,128)(2,1)S(1)}, u32[]{:S(2)}, u32[]{:S(2)}) collective-permute-start(bf16[512,256]{1,0:T(8,128)(2,1)S(1)} %get-tuple-element.219), channel_id=1, source_target_pairs={{0,1},{1,2},{2,3},{3,4},{4,5},{5,6},{6,7},{7,8},{8,9},{9,10},{10,1... | collective-permute-start | bytes 786440 | tf_op jit(solution)/shard_map/while/body/eval_jaxpr/ppermute | solution.py:18
  529.9 9.5 %collective-permute-start = (bf16[512,256]{1,0:T(8,128)(2,1)S(1)}, bf16[512,256]{1,0:T(8,128)(2,1)S(1)}, u32[]{:S(2)}, u32[]{:S(2)}) collective-permute-start(bf16[512,256]{1,0:T(8,128)(2,1)S(1)} %get-tuple-element.219), channel_id=1, source_target_pairs={{0,1},{1,2},{2,3},{3,4},{4,5},{5,6},{6,7},{7,8},{8,9},{9,10},{10,1... | collective-permute-start | bytes 786440 | tf_op jit(solution)/shard_map/while/body/eval_jaxpr/ppermute | solution.py:18
  540.5 9.5 %collective-permute-start = (bf16[512,256]{1,0:T(8,128)(2,1)S(1)}, bf16[512,256]{1,0:T(8,128)(2,1)S(1)}, u32[]{:S(2)}, u32[]{:S(2)}) collective-permute-start(bf16[512,256]{1,0:T(8,128)(2,1)S(1)} %get-tuple-element.219), channel_id=1, source_target_pairs={{0,1},{1,2},{2,3},{3,4},{4,5},{5,6},{6,7},{7,8},{8,9},{9,10},{10,1... | collective-permute-start | bytes 786440 | tf_op jit(solution)/shard_map/while/body/eval_jaxpr/ppermute | solution.py:18
  551.1 9.5 %collective-permute-start = (bf16[512,256]{1,0:T(8,128)(2,1)S(1)}, bf16[512,256]{1,0:T(8,128)(2,1)S(1)}, u32[]{:S(2)}, u32[]{:S(2)}) collective-permute-start(bf16[512,256]{1,0:T(8,128)(2,1)S(1)} %get-tuple-element.219), channel_id=1, source_target_pairs={{0,1},{1,2},{2,3},{3,4},{4,5},{5,6},{6,7},{7,8},{8,9},{9,10},{10,1... | collective-permute-start | bytes 786440 | tf_op jit(solution)/shard_map/while/body/eval_jaxpr/ppermute | solution.py:18
  561.6 9.5 %collective-permute-start = (bf16[512,256]{1,0:T(8,128)(2,1)S(1)}, bf16[512,256]{1,0:T(8,128)(2,1)S(1)}, u32[]{:S(2)}, u32[]{:S(2)}) collective-permute-start(bf16[512,256]{1,0:T(8,128)(2,1)S(1)} %get-tuple-element.219), channel_id=1, source_target_pairs={{0,1},{1,2},{2,3},{3,4},{4,5},{5,6},{6,7},{7,8},{8,9},{9,10},{10,1... | collective-permute-start | bytes 786440 | tf_op jit(solution)/shard_map/while/body/eval_jaxpr/ppermute | solution.py:18
  572.2 9.5 %collective-permute-start = (bf16[512,256]{1,0:T(8,128)(2,1)S(1)}, bf16[512,256]{1,0:T(8,128)(2,1)S(1)}, u32[]{:S(2)}, u32[]{:S(2)}) collective-permute-start(bf16[512,256]{1,0:T(8,128)(2,1)S(1)} %get-tuple-element.219), channel_id=1, source_target_pairs={{0,1},{1,2},{2,3},{3,4},{4,5},{5,6},{6,7},{7,8},{8,9},{9,10},{10,1... | collective-permute-start | bytes 786440 | tf_op jit(solution)/shard_map/while/body/eval_jaxpr/ppermute | solution.py:18
  582.8 9.5 %collective-permute-start = (bf16[512,256]{1,0:T(8,128)(2,1)S(1)}, bf16[512,256]{1,0:T(8,128)(2,1)S(1)}, u32[]{:S(2)}, u32[]{:S(2)}) collective-permute-start(bf16[512,256]{1,0:T(8,128)(2,1)S(1)} %get-tuple-element.219), channel_id=1, source_target_pairs={{0,1},{1,2},{2,3},{3,4},{4,5},{5,6},{6,7},{7,8},{8,9},{9,10},{10,1... | collective-permute-start | bytes 786440 | tf_op jit(solution)/shard_map/while/body/eval_jaxpr/ppermute | solution.py:18
Sparse Core Ops, SparseCore 0:
  10.5 50.8 all-gather.5
  63.8 47.0 all-gather.3
  112.5 88.4 all-gather.7
  236.0 92.8 reduce-scatter.1
where the time goes:
time: 613 us; the launch traced here: 601 us
  waiting for transfers between devices  278 us (45%)
  matrix products  129 us (21%)
  other arithmetic  125 us (20%)
  local copies, waits for them, and re-layouts  54.1 us (9%)
  between operations  14.1 us (2%)
    ppermute x15, waiting for transfers between devices, from_behind(): return lax.ppermute(value, axis, pairs)  141 us
    scatter-add x1, other arithmetic, step_fn(): running = running.at[key_index.reshape(-1)].add(update)  66.6 us
    all_gather x1, waiting for transfers between devices, on_device(): shard_piece = lax.all_gather(out_grad, 'head', axis=3, tiled=True)  46.3 us
    all_gather x1, waiting for transfers between devices, on_device(): lax.all_gather(key_states, 'ctx', axis=1, tiled=True)  44.4 us
    all_gather x1, waiting for transfers between devices, on_device(): lax.all_gather(value_states, 'ctx', axis=1, tiled=True)  44.2 us
    dot_general x1, matrix products, attend_group(): jnp.einsum('rqhd,rekd->rqhek', grad_rows, value_rows, preferred_element_t...  26.1 us
    dot_general x1, matrix products, attend_group(): jnp.einsum('rqhek,rqhd->rekd', probs_low, grad_rows, preferred_element_ty...  22.5 us
    dot_general x1, matrix products, attend_group(): jnp.einsum('rqhek,rekd->rqhd', probs, value_rows, preferred_element_type=...  20.4 us
  transfers between devices with their start and end apart: 19, of which 18 were waited for; matrix products, arithmetic and copies ran while one was open for 45% of the time, Pallas kernels for 0%

commit v1 on v0

v1 whole, which is shorter than its diff:
```python
import functools
import math

import jax
import jax.numpy as jnp
from jax import lax
from jax.experimental import pallas as pl
from jax.experimental.pallas import tpu as pltpu
from jax.sharding import PartitionSpec as P

HD = 128
NG = 4
BLK = 64
ROWS = 8
NE = 40
EPC = 8
CK = EPC * BLK
NCH = NE // EPC
QN = NG * BLK
CHUNKS = 36
NOSLOT = CHUNKS * EPC
SCALE = 1.0 / math.sqrt(HD)
LOG2E = 1.4426950408889634
FAR = -1e30


def chunk_base(i):
    return jnp.where(i == 0, 0, jnp.where(i == 1, 2, 5 * i - 4))


def chunk_count(i):
    return jnp.minimum(NCH, 2 * (i + 1))


def lists(vertical, slash, me, n_ctx):
    rows = jnp.arange(ROWS, dtype=jnp.int32)
    bid = rows * n_ctx + me
    raw = jnp.concatenate([bid[:, None] - slash, vertical], axis=1)
    kept = (raw >= 0) & (raw <= bid[:, None])
    order = jnp.arange(NE, dtype=jnp.int32)
    place = jnp.sum((kept[:, None, :] & (order[None, None, :] < order[None, :, None])).astype(jnp.int32), axis=2)
    place = jnp.where(kept, place, NE)
    here = place[:, None, :] == order[None, :, None]
    moved = raw % n_ctx * ROWS + raw // n_ctx
    index = jnp.sum(jnp.where(here, moved[:, None, :], 0), axis=2)
    far = jnp.where(jnp.any(here, axis=2), 0.0, FAR).astype(jnp.float32)
    slot = chunk_base(rows)[:, None] * EPC + place
    block = jnp.arange(ROWS * n_ctx, dtype=jnp.int32)
    hit = (raw[:, None, :] == block[None, :, None]) & kept[:, None, :]
    where = NOSLOT + jnp.sum(jnp.where(hit, slot[:, None, :] - NOSLOT, 0), axis=2)
    return index, far, where


def dot(a, b, ca, cb):
    return lax.dot_general(a, b, (((ca,), (cb,)), ((), ())), preferred_element_type=jnp.float32)


def heads_down(x):
    return jnp.concatenate([x[:, h * HD:(h + 1) * HD] for h in range(NG)], axis=0)


def heads_across(x):
    return jnp.concatenate([x[h * BLK:(h + 1) * BLK] for h in range(NG)], axis=1)


def forward_row(i, index, far, q, kv, s):
    qs = heads_down(q[i])
    s.qs[i] = qs
    base, count = chunk_base(i), chunk_count(i)
    key_pos = lax.broadcasted_iota(jnp.int32, (BLK, QN), 0)
    query_pos = lax.broadcasted_iota(jnp.int32, (BLK, QN), 1) % BLK

    def scores(ch, top, first):
        for e in range(EPC):
            s.kvrow[ch, e * BLK:(e + 1) * BLK, :] = kv[index[i, ch * EPC + e]]
        sc = dot(s.kvrow[ch, :, :HD], qs, 1, 1)
        for e in range(EPC):
            part = sc[e * BLK:(e + 1) * BLK]
            if first and e == 0:
                part = jnp.where(key_pos <= query_pos, part, FAR)
            s.sc[ch, e * BLK:(e + 1) * BLK, :] = part
            part = jnp.max(part.reshape(BLK // 8, 8, QN), axis=0)
            top = jnp.maximum(top, part + far[i, ch * EPC + e])
        return top

    top = scores(0, jnp.full((8, QN), FAR, jnp.float32), True)
    top = lax.fori_loop(1, count, lambda ch, t: scores(ch, t, False), top)
    top = jnp.max(top, axis=0, keepdims=True) * (SCALE * LOG2E)

    def values(ch, carry):
        total, acc = carry
        for e in range(EPC):
            shift = top - far[i, ch * EPC + e]
            p = jnp.exp2(s.sc[ch, e * BLK:(e + 1) * BLK, :] * (SCALE * LOG2E) - shift)
            total = total + jnp.sum(p.reshape(BLK // 8, 8, QN), axis=0)
            s.p[base + ch, e * BLK:(e + 1) * BLK, :] = p.astype(jnp.bfloat16)
        acc = acc + dot(s.kvrow[ch, :, HD:], s.p[base + ch], 0, 0)
        return total, acc

    total, acc = lax.fori_loop(
        0, count, values, (jnp.zeros((8, QN), jnp.float32), jnp.zeros((HD, QN), jnp.float32))
    )
    inv = 1.0 / jnp.sum(total, axis=0, keepdims=True)
    out = (acc * inv).astype(jnp.bfloat16)
    s.ot[i] = out
    s.inv[i] = jnp.broadcast_to(inv, (8, QN))
    s.att[i] = heads_across(out.astype(jnp.float32).T.astype(jnp.bfloat16))


def backward_row(i, index, g, kv, s):
    base, count = chunk_base(i), chunk_count(i)
    gt = heads_down(g[i].astype(jnp.float32)).T
    gt = (gt * s.inv[i][0:1]).astype(jnp.bfloat16)
    g32 = gt.astype(jnp.float32)
    delta = jnp.sum(g32 * s.ot[i].astype(jnp.float32), axis=0, keepdims=True)
    s.gt[...] = gt
    s.gs[...] = g32.T.astype(jnp.bfloat16)

    def chunk(ch, acc):
        for e in range(EPC):
            s.kvrow[0, e * BLK:(e + 1) * BLK, :] = kv[index[i, ch * EPC + e]]
        dp = dot(s.kvrow[0, :, HD:], s.gt[...], 1, 0)
        p = s.p[base + ch]
        ds = (p.astype(jnp.float32) * (dp - delta)).astype(jnp.bfloat16)
        start = (base + ch) * EPC
        dk = dot(ds, s.qs[i], 1, 0)
        dv = dot(p, s.gs[...], 1, 0)
        s.slots[pl.ds(start, EPC), :, :HD] = dk.reshape(EPC, BLK, HD)
        s.slots[pl.ds(start, EPC), :, HD:] = dv.reshape(EPC, BLK, HD)
        return acc + dot(s.kvrow[0, :, :HD], ds, 0, 0)

    acc = lax.fori_loop(0, count, chunk, jnp.zeros((HD, QN), jnp.float32))
    s.dq[i] = heads_across((acc * SCALE).T).astype(jnp.bfloat16)


def collect(i, u, where, s):
    def more(r, acc):
        return acc + s.slots[where[r, u]]

    return lax.fori_loop(i, ROWS, more, jnp.zeros((BLK, 2 * HD), jnp.float32))


class Scratch:
    pass


MESH = pl.DeviceIdType.MESH
OG_PARTS = 4
OG_ROWS = ROWS // OG_PARTS
KV_PARTS = 2
KV_ROWS = ROWS // KV_PARTS


def send(src, dst, send_sem, recv_sem, device):
    pltpu.make_async_remote_copy(
        src_ref=src, dst_ref=dst, send_sem=send_sem, recv_sem=recv_sem, device_id=device, device_id_type=MESH
    ).start()


def sent(src, sem, device):
    pltpu.make_async_remote_copy(
        src_ref=src, dst_ref=src, send_sem=sem, recv_sem=sem, device_id=device, device_id_type=MESH
    ).wait_send()


def arrived(dst, sem, device):
    pltpu.make_async_remote_copy(
        src_ref=dst, dst_ref=dst, send_sem=sem, recv_sem=sem, device_id=device, device_id_type=MESH
    ).wait_recv()


class Place:
    def __init__(self):
        h, c = lax.axis_index("head"), lax.axis_index("ctx")
        self.h, self.c = h, c
        x, zl = h // 2, h % 2
        y, zh, core = c // 4, c // 2 % 2, c % 2
        self.y, self.zh, self.core = y, zh, core
        self.xp, self.xm, self.xo = [(x + k) % 4 * 2 + zl for k in (1, 3, 2)]
        self.zp = x * 2 + 1 - zl
        flip = 1 - 2 * zl
        self.xp_z, self.xm_z, self.xo_z = self.xp + flip, self.xm + flip, self.xo + flip
        self.ys = [(y + k) % 4 for k in (1, 3, 2)]
        self.yp, self.ym, self.yo = [v * 4 + zh * 2 + core for v in self.ys]
        turn = 2 * (1 - 2 * zh)
        self.zhp = c + turn
        self.yp_z, self.ym_z, self.yo_z = self.yp + turn, self.ym + turn, self.yo + turn
        self.other = 1 - 2 * core
        self.sib = c + self.other

    def on_head(self, index):
        return (index, self.c)

    def on_ctx(self, index):
        return (self.h, index)


def gather_out_grad(me, s):
    def piece(owner, k):
        return s.og.at[owner, pl.ds(k * OG_ROWS, OG_ROWS)]

    def go(kind, owner, to, k):
        ref = piece(owner, k)
        send(ref, ref, s.og_send.at[kind, k], s.og_recv.at[kind, k], me.on_head(to))

    def come(kind, owner, k):
        arrived(piece(owner, k), s.og_recv.at[kind, k], me.on_head(me.zp))

    def gone(kind, owner, k):
        sent(piece(owner, k), s.og_send.at[kind, k], me.on_head(me.zp))

    return go, come, gone


def gather_kv(me, s):
    def piece(owner, k):
        return s.kv.at[pl.ds(owner * ROWS + k * KV_ROWS, KV_ROWS)]

    def go(kind, owner, to, k):
        ref = piece(owner, k)
        send(ref, ref, s.kv_send.at[kind, k], s.kv_recv.at[kind, k], me.on_ctx(to))

    def come(kind, owner, k):
        arrived(piece(owner, k), s.kv_recv.at[kind, k], me.on_ctx(me.sib))

    def gone(kind, owner, k):
        sent(piece(owner, k), s.kv_send.at[kind, k], me.on_ctx(me.sib))

    return go, come, gone


def project_grad(owner, first, weight, s):
    cols = pl.ds(pl.multiple_of(owner * NG * HD, NG * HD), NG * HD)
    part = dot(s.og[owner].reshape(ROWS * BLK, NG * HD), weight[:, cols], 1, 1)
    for half in range(2):
        now = part[:, half * 2 * HD:(half + 1) * 2 * HD].reshape(ROWS, BLK, 2 * HD)
        at = slice(half * ROWS, (half + 1) * ROWS)
        s.slots[at] = now if first else s.slots[at] + now


def layer_kernel(n_ctx, index, far, where, q, key, value, out_grad, weight, layer_out, dq, dk, dv, *refs):
    s = Scratch()
    (
        s.qs, s.kvrow, s.sc, s.p, s.ot, s.inv, s.gt, s.gs, s.slots, s.att, s.g, s.kv, s.og,
        s.lo, s.s1, s.r1, s.s2, s.r2, s.s3, s.r3,
        s.og_send, s.og_recv, s.kv_send, s.kv_recv, s.lo_send, s.lo_recv,
        s.send1, s.recv1, s.send2, s.recv2, s.send3, s.recv3,
    ) = refs
    s.dq = dq
    me = Place()
    mine = pl.multiple_of(me.c * ROWS, ROWS)
    s.kv[pl.ds(mine, ROWS), :, :HD] = key[...]
    s.kv[pl.ds(mine, ROWS), :, HD:] = value[...]
    s.og[me.h] = out_grad[...]

    barrier = pltpu.get_barrier_semaphore()
    partners = [me.on_head(d) for d in (me.xp, me.xm, me.xo, me.zp)]
    partners += [me.on_ctx(d) for d in (me.zhp, me.yp, me.ym, me.yo, me.sib)]
    for device in partners:
        pl.semaphore_signal(barrier, inc=1, device_id=device, device_id_type=MESH)
    pl.semaphore_wait(barrier, len(partners))

    og_go, og_come, og_gone = gather_out_grad(me, s)
    kv_go, kv_come, kv_gone = gather_kv(me, s)
    kv_kinds = [
        (0, me.c, me.yp), (1, me.c, me.ym), (2, me.c, me.yo), (3, me.c, me.zhp),
        (4, me.zhp, me.yp), (5, me.zhp, me.ym), (6, me.zhp, me.yo),
        (7, me.c, me.sib), (8, me.zhp, me.sib), (9, me.ym, me.sib), (10, me.yp, me.sib), (11, me.yo, me.sib),
        (12, me.ym_z, me.sib), (13, me.yp_z, me.sib), (14, me.yo_z, me.sib),
    ]
    og_kinds = [
        (0, me.h, me.xp), (1, me.h, me.xm), (2, me.h, me.xo), (3, me.h, me.zp),
        (4, me.zp, me.xp), (5, me.zp, me.xm), (6, me.xo, me.zp),
    ]

    def kv_start(kinds, k):
        for kind in kinds:
            kv_go(*kv_kinds[kind], k)

    def og_start(kinds, k):
        for kind in kinds:
            og_go(*og_kinds[kind], k)

    @pl.loop(0, KV_PARTS)
    def _(k):
        kv_start((3, 0, 1, 2, 7), k)

    @pl.loop(0, OG_PARTS)
    def _(k):
        og_start((3,), k)

    @pl.loop(0, OG_PARTS)
    def _(k):
        og_start((0, 1, 2), k)

    s.slots[NOSLOT] = jnp.zeros((BLK, 2 * HD), jnp.float32)
    project_grad(me.h, True, weight, s)

    @pl.loop(0, KV_PARTS)
    def _(k):
        kv_come(3, me.zhp, k)
        kv_start((4, 5, 6, 8), k)

    @pl.loop(0, OG_PARTS)
    def _(k):
        og_come(3, me.zp, k)
        og_start((4, 5), k)

    project_grad(me.zp, False, weight, s)

    @pl.loop(0, KV_PARTS)
    def _(k):
        for kind, owner in ((0, me.ym), (1, me.yp), (2, me.yo)):
            kv_come(kind, owner, k)
            kv_start((kind + 9,), k)

    @pl.loop(0, OG_PARTS)
    def _(k):
        og_come(2, me.xo, k)
        og_start((6,), k)

    @pl.loop(0, KV_PARTS)
    def _(k):
        for kind, owner in ((4, me.ym_z), (5, me.yp_z), (6, me.yo_z)):
            kv_come(kind, owner, k)
            kv_start((kind + 8,), k)

    @pl.loop(0, KV_PARTS)
    def _(k):
        owners = (me.c, me.zhp, me.ym, me.yp, me.yo, me.ym_z, me.yp_z, me.yo_z)
        for kind, owner in enumerate(owners, 7):
            kv_come(kind, owner + me.other, k)

    project_grad(me.xo, False, weight, s)

    @pl.loop(0, ROWS)
    def _(i):
        forward_row(i, index, far, q, s.kv, s)

    for kind, owner in ((0, me.xm), (1, me.xp), (4, me.xm_z), (5, me.xp_z), (6, me.xo_z)):

        @pl.loop(0, OG_PARTS)
        def _(k):
            og_come(kind, owner, k)

        project_grad(owner, False, weight, s)

    @pl.loop(0, ROWS)
    def _(i):
        s.g[i, :, :2 * HD] = s.slots[i].astype(jnp.bfloat16)
        s.g[i, :, 2 * HD:] = s.slots[ROWS + i].astype(jnp.bfloat16)

    @pl.loop(0, OG_PARTS)
    def _(k):
        for kind, owner, to in og_kinds:
            og_gone(kind, owner, k)

    @pl.loop(0, KV_PARTS)
    def _(k):
        for kind, owner, to in kv_kinds:
            kv_gone(kind, owner, k)

    lo_kinds = [
        (0, me.xo_z, me.zp), (1, me.xp_z, me.xp), (2, me.xm_z, me.xm),
        (3, me.xp, me.xp), (4, me.xm, me.xm), (5, me.xo, me.xo), (6, me.zp, me.zp),
    ]

    def lo_piece(owner, k):
        return s.og.at[owner, pl.ds(k * OG_ROWS, OG_ROWS)]

    def lo_slot(kind, k):
        return s.lo.at[kind, pl.ds(k * OG_ROWS, OG_ROWS)]

    def lo_start(kind, k):
        _, owner, to = lo_kinds[kind]
        send(lo_piece(owner, k), lo_slot(kind, k), s.lo_send.at[kind, k], s.lo_recv.at[kind, k], me.on_head(to))

    def lo_come(kind, k):
        arrived(lo_slot(kind, k), s.lo_recv.at[kind, k], me.on_head(me.zp))
        return lo_slot(kind, k)[...].astype(jnp.float32)

    def share(owner, k):
        cols = pl.ds(pl.multiple_of(owner * NG * HD, NG * HD), NG * HD)
        rows = s.att[pl.ds(k * OG_ROWS, OG_ROWS)].reshape(OG_ROWS * BLK, NG * HD)
        out = dot(rows, weight[:, cols], 1, 0).astype(jnp.bfloat16)
        s.og[owner, pl.ds(k * OG_ROWS, OG_ROWS)] = out.reshape(OG_ROWS, BLK, NG * HD)

    @pl.loop(0, OG_PARTS)
    def _(k):
        for kind in range(5):
            share(lo_kinds[kind][1], k)
            lo_start(kind, k)
        share(me.xo, k)
        share(me.zp, k)
        share(me.h, k)

    def lo_pass(k):
        at = pl.ds(k * OG_ROWS, OG_ROWS)
        s.og[me.xo, at] = (s.og[me.xo, at].astype(jnp.float32) + lo_come(0, k)).astype(jnp.bfloat16)
        lo_start(5, k)
        total = s.og[me.zp, at].astype(jnp.float32) + lo_come(1, k) + lo_come(2, k)
        s.og[me.zp, at] = total.astype(jnp.bfloat16)
        lo_start(6, k)

    def lo_final(k):
        at = pl.ds(k * OG_ROWS, OG_ROWS)
        total = s.og[me.h, at].astype(jnp.float32)
        for kind in (3, 4, 5, 6):
            total = total + lo_come(kind, k)
        layer_out[at] = total.astype(jnp.bfloat16)

    def kv_first(i):
        @pl.loop(0, n_ctx // 2)
        def _(j):
            u = i * n_ctx + 2 * j + 1 - me.core
            s.s1[i, j] = collect(i, u, where, s).astype(jnp.bfloat16)

        send(s.s1.at[i], s.r1.at[i], s.send1.at[i], s.recv1.at[i], me.on_ctx(me.sib))

    def kv_second(i):
        arrived(s.r1.at[i], s.recv1.at[i], me.on_ctx(me.sib))

        @pl.loop(0, n_ctx // 2)
        def _(j):
            u = i * n_ctx + 2 * j + me.core
            s.s2[i, j] = (collect(i, u, where, s) + s.r1[i, j].astype(jnp.float32)).astype(jnp.bfloat16)

        for kind, to in enumerate((me.yp, me.ym, me.yo)):
            src = s.s2.at[i, pl.ds(2 * me.ys[kind], 2)]
            send(src, s.r2.at[i, kind], s.send2.at[i, kind], s.recv2.at[i, kind], me.on_ctx(to))

    def kv_sum(i, zh):
        total = s.s2[i, 2 * me.y + zh].astype(jnp.float32)
        for kind in range(3):
            total = total + s.r2[i, kind, zh].astype(jnp.float32)
        return total

    def kv_third(i):
        for kind in range(3):
            arrived(s.r2.at[i, kind], s.recv2.at[i, kind], me.on_ctx(me.sib))
        s.s3[i] = kv_sum(i, 1 - me.zh).astype(jnp.bfloat16)
        send(s.s3.at[i], s.r3.at[i], s.send3.at[i], s.recv3.at[i], me.on_ctx(me.zhp))

    def kv_final(i):
        arrived(s.r3.at[i], s.recv3.at[i], me.on_ctx(me.sib))
        total = kv_sum(i, me.zh) + s.r3[i].astype(jnp.float32)
        dk[i] = (total[:, :HD] * SCALE).astype(jnp.bfloat16)
        dv[i] = total[:, HD:].astype(jnp.bfloat16)

    @pl.loop(0, ROWS + 3)
    def _(n):
        i = ROWS - 1 - n

        @pl.when(n < ROWS)
        def _():
            backward_row(i, index, s.g, s.kv, s)
            kv_first(i)

        @pl.when((n >= 1) & (n <= ROWS))
        def _():
            kv_second(i + 1)

        @pl.when((n >= 2) & (n <= ROWS + 1))
        def _():
            kv_third(i + 2)

        @pl.when(n >= 3)
        def _():
            kv_final(i + 3)

        @pl.when((n >= 1) & (n <= OG_PARTS))
        def _():
            lo_pass(n - 1)

        @pl.when((n >= ROWS + 3 - OG_PARTS))
        def _():
            lo_final(n - (ROWS + 3 - OG_PARTS))

    @pl.loop(0, OG_PARTS)
    def _(k):
        for kind, owner, to in lo_kinds:
            sent(lo_piece(owner, k), s.lo_send.at[kind, k], me.on_head(to))

    @pl.loop(0, ROWS)
    def _(i):
        sent(s.s1.at[i], s.send1.at[i], me.on_ctx(me.sib))
        for kind in range(3):
            sent(s.s2.at[i, pl.ds(0, 2)], s.send2.at[i, kind], me.on_ctx(me.sib))
        sent(s.s3.at[i], s.send3.at[i], me.on_ctx(me.zhp))


def layer(index, far, where, q, key, value, out_grad, weight, n_head, n_ctx):
    smem = pl.BlockSpec(memory_space=pltpu.SMEM)
    vmem = pl.BlockSpec(memory_space=pltpu.VMEM)
    wide, narrow = (ROWS, BLK, NG * HD), (ROWS, BLK, HD)
    low = jnp.bfloat16
    sem = pltpu.SemaphoreType.DMA
    return pl.pallas_call(
        functools.partial(layer_kernel, n_ctx),
        out_shape=[jax.ShapeDtypeStruct(shape, low) for shape in (wide, wide, narrow, narrow)],
        in_specs=[smem] * 3 + [vmem] * 5,
        out_specs=[vmem] * 4,
        scratch_shapes=[
            pltpu.VMEM((ROWS, QN, HD), low),
            pltpu.VMEM((NCH, CK, 2 * HD), low),
            pltpu.VMEM((NCH, CK, QN), jnp.float32),
            pltpu.VMEM((CHUNKS, CK, QN), low),
            pltpu.VMEM((ROWS, HD, QN), low),
            pltpu.VMEM((ROWS, 8, QN), jnp.float32),
            pltpu.VMEM((HD, QN), low),
            pltpu.VMEM((QN, HD), low),
            pltpu.VMEM((NOSLOT + 1, BLK, 2 * HD), jnp.float32),
            pltpu.VMEM(wide, low),
            pltpu.VMEM(wide, low),
            pltpu.VMEM((n_ctx * ROWS, BLK, 2 * HD), low),
            pltpu.VMEM((n_head,) + wide, low),
            pltpu.VMEM((7,) + wide, low),
            pltpu.VMEM((ROWS, n_ctx // 2, BLK, 2 * HD), low),
            pltpu.VMEM((ROWS, n_ctx // 2, BLK, 2 * HD), low),
            pltpu.VMEM((ROWS, n_ctx // 2, BLK, 2 * HD), low),
            pltpu.VMEM((ROWS, 3, 2, BLK, 2 * HD), low),
            pltpu.VMEM((ROWS, BLK, 2 * HD), low),
            pltpu.VMEM((ROWS, BLK, 2 * HD), low),
            sem((7, OG_PARTS)), sem((7, OG_PARTS)),
            sem((15, KV_PARTS)), sem((15, KV_PARTS)),
            sem((7, OG_PARTS)), sem((7, OG_PARTS)),
            sem((ROWS,)), sem((ROWS,)),
            sem((ROWS, 3)), sem((ROWS, 3)),
            sem((ROWS,)), sem((ROWS,)),
        ],
        compiler_params=pltpu.CompilerParams(
            vmem_limit_bytes=63 << 20, collective_id=0, has_side_effects=True
        ),
        name="layer",
    )(index, far, where, q, key, value, out_grad, weight)


def on_device(query, key, value, out_grad, weight, vertical, slash):
    n_head, n_ctx = lax.axis_size("head"), lax.axis_size("ctx")
    index, far, where = lists(vertical[0, :, 0], slash[0, :, 0], lax.axis_index("ctx"), n_ctx)
    outs = layer(
        index, far, where, query[:, 0], key[:, 0], value[:, 0], out_grad[:, 0], weight, n_head, n_ctx
    )
    return tuple(x[:, None] for x in outs)


def solution(mesh):
    spread = P(None, "ctx", None, "head")
    listed = P("head", None, "ctx", None)
    return jax.shard_map(
        on_device,
        mesh=mesh,
        in_specs=(spread, spread, spread, spread, P("head", None), listed, listed),
        out_specs=(spread,) * 4,
        check_vma=False,
    )
```

time: 613 us -> 125 us (0.20); the launches traced: 601 us -> 123 us
  waiting for transfers between devices: 278 us -> 0 us
  matrix products: 129 us -> 0 us
  other arithmetic: 125 us -> 4.26 us
  Pallas kernels: 0 us -> 112 us
  local copies, waits for them, and re-layouts: 54.1 us -> 6.87 us
  between operations: 14.1 us -> 0.68 us
    ppermute x15 -> x0, waiting for transfers between devices: 141 us -> none  [from_behind(): return lax.ppermute(value, axis, pairs)]
    all_gather x3 -> x0, waiting for transfers between devices: 135 us -> none  [the longest x1 46.3 us: on_device(): shard_piece = lax.all_gather(out_grad, 'head', axis=3, tiled=True)]
    dot_general x8 -> x0, matrix products: 129 us -> none  [the longest x1 26.1 us: attend_group(): jnp.einsum('rqhd,rekd->rqhek', grad_rows, value_rows, preferred_element_t...]
    pallas_call x0 -> x1, Pallas kernels: none -> 112 us  [layer(): pl.pallas_call(functools.partial(layer_kernel, n_ctx), out_shape=[jax.Sha...]
    scatter-add x1 -> x0, other arithmetic: 66.6 us -> none  [step_fn(): running = running.at[key_index.reshape(-1)].add(update)]
    reduce_sum x1 -> x3, other arithmetic: 19 us -> 1.24 us  [the longest x1 0.82 us: lists(): index = jnp.sum(jnp.where(here, moved[:, None, :], 0), axis=2)]
    another operation x1 -> x0, other arithmetic: 16.5 us -> none  [step_fn(): jnp.stack([key_part, value_part], axis=3).reshape(-1, block_rows, 2, HD)]
    add x17 -> x2, other arithmetic: 16.5 us -> 0.6 us  [the longest x1 0.6 us: lists(): NOSLOT + jnp.sum(jnp.where(hit, slot[:, None, :] - NOSLOT, 0), axis=2)]
  transfers between devices with their start and end apart: 19 -> 0, of which waited for: 18 -> 0; matrix products, arithmetic and copies ran while one was open for 45% -> 0% of each run, Pallas kernels for 0% -> 0%
where the time goes in v1:
time: 125 us; the launch traced here: 123 us
  Pallas kernels  112 us (90%)
  local copies, waits for them, and re-layouts  6.87 us (5%)
  other arithmetic  4.26 us (3%)
    pallas_call x1, Pallas kernels, layer(): pl.pallas_call(functools.partial(layer_kernel, n_ctx), out_shape=[jax.Sha...  112 us
    unnamed x4, local copies, waits for them, and re-layouts  6.87 us

profile of v1, /device:TPU:2, one launch (start us, length us, event | category | flops | bytes accessed | tf_op | source)
XLA Modules:
  0.0 123.5 jit_solution(7841624404801505451)
XLA Ops:
  0.7 0.8 broadcast_subtract_fusion
  1.4 0.8 compare_and_fusion
  2.2 0.2 convert_reduce_fusion
  2.4 0.1 add_add_fusion
  2.5 0.2 select_reduce_fusion
  2.7 0.6 broadcast_add_fusion.where
  3.3 0.2 fusion
  3.5 0.8 select_reduce_fusion.1.index
  4.3 0.6 broadcast_select_fusion.far
  4.9 111.7 %layer.1 = (bf16[8,64,512]{2,1,0:T(8,128)(2,1)}, bf16[8,64,512]{2,1,0:T(8,128)(2,1)}, bf16[8,64,128]{2,1,0:T(8,128)(2,1)}, bf16[8,64,128]{2,1,0:T(8,128)(2,1)}) custom-call(s32[8,40]{1,0:T(8,128)} %select_reduce_fusion.1.index, f32[8,40]{1,0:T(8,128)} %broadcast_select_fusion.far, s32[8,128]{1,0:T(8,128)} %broadcast_add_fusion.where, ...), custom_call_target="tpu_custom_call" | custom-call | tf_op jit(solution)/shard_map/layer/pallas_call | solution.py:498
  116.6 1.9 %copy.23 = bf16[8,1,64,512]{3,2,1,0:T(8,128)(2,1)} copy(bf16[8,1,64,512]{3,2,1,0:T(8,128)(2,1)} %bitcast.21) | data formatting | bytes 1048576
  118.5 1.9 %copy.24 = bf16[8,1,64,512]{3,2,1,0:T(8,128)(2,1)} copy(bf16[8,1,64,512]{3,2,1,0:T(8,128)(2,1)} %bitcast.20) | data formatting | bytes 1048576
  120.3 1.6 %copy.25 = bf16[8,1,64,128]{3,2,1,0:T(8,128)(2,1)} copy(bf16[8,1,64,128]{3,2,1,0:T(8,128)(2,1)} %bitcast.25) | data formatting | bytes 262144
  121.9 1.6 %copy.26 = bf16[8,1,64,128]{3,2,1,0:T(8,128)(2,1)} copy(bf16[8,1,64,128]{3,2,1,0:T(8,128)(2,1)} %bitcast.24) | data formatting | bytes 262144
  (3 shorter events, 0.0 us)

commit v2 on v1

v2 whole, which is shorter than its diff:
```python
import functools
import math

import jax
import jax.numpy as jnp
from jax import lax
from jax.experimental import pallas as pl
from jax.experimental.pallas import tpu as pltpu
from jax.sharding import PartitionSpec as P

HD = 128
NG = 4
BLK = 64
ROWS = 8
NE = 40
EPC = 8
CK = EPC * BLK
NCH = NE // EPC
QN = NG * BLK
CHUNKS = 36
NOSLOT = CHUNKS * EPC
SCALE = 1.0 / math.sqrt(HD)
LOG2E = 1.4426950408889634
FAR = -1e30


def chunk_base(i):
    return jnp.where(i == 0, 0, jnp.where(i == 1, 2, 5 * i - 4))


def lists(vertical, slash, me, n_ctx):
    rows = jnp.arange(ROWS, dtype=jnp.int32)
    bid = rows * n_ctx + me
    raw = jnp.concatenate([bid[:, None] - slash, vertical], axis=1)
    kept = (raw >= 0) & (raw <= bid[:, None])
    order = jnp.arange(NE, dtype=jnp.int32)
    place = jnp.sum((kept[:, None, :] & (order[None, None, :] < order[None, :, None])).astype(jnp.int32), axis=2)
    place = jnp.where(kept, place, NE)
    here = place[:, None, :] == order[None, :, None]
    moved = raw % n_ctx * ROWS + raw // n_ctx
    index = jnp.sum(jnp.where(here, moved[:, None, :], 0), axis=2)
    far = jnp.where(jnp.any(here, axis=2), 0.0, FAR).astype(jnp.float32)
    slot = chunk_base(rows)[:, None] * EPC + place
    block = jnp.arange(ROWS * n_ctx, dtype=jnp.int32)
    hit = (raw[:, None, :] == block[None, :, None]) & kept[:, None, :]
    where = NOSLOT + jnp.sum(jnp.where(hit, slot[:, None, :] - NOSLOT, 0), axis=2)
    return index, far, where


def dot(a, b, ca, cb):
    return lax.dot_general(a, b, (((ca,), (cb,)), ((), ())), preferred_element_type=jnp.float32)


def heads_down(x):
    return jnp.concatenate([x[:, h * HD:(h + 1) * HD] for h in range(NG)], axis=0)


def heads_across(x):
    return jnp.concatenate([x[h * BLK:(h + 1) * BLK] for h in range(NG)], axis=1)


def forward_row(i, count, index, far, q, s):
    qs = heads_down(q[i])
    s.qs[i] = qs
    base = chunk_base(i)
    key_pos = lax.broadcasted_iota(jnp.int32, (BLK, QN), 0)
    query_pos = lax.broadcasted_iota(jnp.int32, (BLK, QN), 1) % BLK
    top = jnp.full((8, QN), FAR, jnp.float32)
    for ch in range(count):
        for e in range(EPC):
            s.kvrow[ch, e * BLK:(e + 1) * BLK, :] = s.table[index[i, ch * EPC + e]]
        sc = dot(s.kvrow[ch, :, :HD], qs, 1, 1)
        for e in range(EPC):
            part = sc[e * BLK:(e + 1) * BLK]
            if ch == 0 and e == 0:
                part = jnp.where(key_pos <= query_pos, part, FAR)
            s.sc[ch, e * BLK:(e + 1) * BLK, :] = part
            part = jnp.max(part.reshape(BLK // 8, 8, QN), axis=0)
            top = jnp.maximum(top, part + far[i, ch * EPC + e])
    top = jnp.max(top, axis=0, keepdims=True) * (SCALE * LOG2E)

    total = jnp.zeros((8, QN), jnp.float32)
    acc = jnp.zeros((HD, QN), jnp.float32)
    for ch in range(count):
        for e in range(EPC):
            shift = top - far[i, ch * EPC + e]
            p = jnp.exp2(s.sc[ch, e * BLK:(e + 1) * BLK, :] * (SCALE * LOG2E) - shift)
            total = total + jnp.sum(p.reshape(BLK // 8, 8, QN), axis=0)
            s.p[base + ch, e * BLK:(e + 1) * BLK, :] = p.astype(jnp.bfloat16)
        acc = acc + dot(s.kvrow[ch, :, HD:], s.p[base + ch], 0, 0)
    inv = 1.0 / jnp.sum(total, axis=0, keepdims=True)
    out = (acc * inv).astype(jnp.bfloat16)
    s.ot[i] = out
    s.inv[i] = jnp.broadcast_to(inv, (8, QN))
    s.att[i] = heads_across(out.astype(jnp.float32).T.astype(jnp.bfloat16))


def backward_row(i, count, index, s):
    base = chunk_base(i)
    gt = heads_down(s.g[i].astype(jnp.float32)).T
    gt = (gt * s.inv[i][0:1]).astype(jnp.bfloat16)
    g32 = gt.astype(jnp.float32)
    delta = jnp.sum(g32 * s.ot[i].astype(jnp.float32), axis=0, keepdims=True)
    gs = g32.T.astype(jnp.bfloat16)
    qs = s.qs[i]
    acc = jnp.zeros((HD, QN), jnp.float32)
    for ch in range(count):
        for e in range(EPC):
            s.kvrow[ch, e * BLK:(e + 1) * BLK, :] = s.table[index[i, ch * EPC + e]]
        dp = dot(s.kvrow[ch, :, HD:], gt, 1, 0)
        p = s.p[base + ch]
        ds = (p.astype(jnp.float32) * (dp - delta)).astype(jnp.bfloat16)
        at = pl.ds((base + ch) * EPC, EPC)
        s.slots[at, :, :HD] = dot(ds, qs, 1, 0).astype(jnp.bfloat16).reshape(EPC, BLK, HD)
        s.slots[at, :, HD:] = dot(p, gs, 1, 0).astype(jnp.bfloat16).reshape(EPC, BLK, HD)
        acc = acc + dot(s.kvrow[ch, :, :HD], ds, 0, 0)
    s.dq[i] = heads_across((acc * SCALE).T).astype(jnp.bfloat16)


def collect(i, u, where, s):
    def more(r, acc):
        return acc + s.slots[where[r, u]].astype(jnp.float32)

    return lax.fori_loop(i, ROWS, more, jnp.zeros((BLK, 2 * HD), jnp.float32))


class Scratch:
    pass


MESH = pl.DeviceIdType.MESH
OG_PARTS = 4
OG_ROWS = ROWS // OG_PARTS
HELD = 4
KV_PARTS = 4
KV_ROWS = ROWS // KV_PARTS


def send(src, dst, send_sem, recv_sem, device):
    pltpu.make_async_remote_copy(
        src_ref=src, dst_ref=dst, send_sem=send_sem, recv_sem=recv_sem, device_id=device, device_id_type=MESH
    ).start()


def sent(src, sem, device):
    pltpu.make_async_remote_copy(
        src_ref=src, dst_ref=src, send_sem=sem, recv_sem=sem, device_id=device, device_id_type=MESH
    ).wait_send()


def arrived(dst, sem, device):
    pltpu.make_async_remote_copy(
        src_ref=dst, dst_ref=dst, send_sem=sem, recv_sem=sem, device_id=device, device_id_type=MESH
    ).wait_recv()


class Place:
    def __init__(self):
        h, c = lax.axis_index("head"), lax.axis_index("ctx")
        self.h, self.c = h, c
        x, zl = h // 2, h % 2
        y, zh, core = c // 4, c // 2 % 2, c % 2
        self.y, self.zh, self.core = y, zh, core
        self.xp, self.xm, self.xo = [(x + k) % 4 * 2 + zl for k in (1, 3, 2)]
        self.zp = x * 2 + 1 - zl
        flip = 1 - 2 * zl
        self.xp_z, self.xm_z, self.xo_z = self.xp + flip, self.xm + flip, self.xo + flip
        self.ys = [(y + k) % 4 for k in (1, 3, 2)]
        self.yp, self.ym, self.yo = [v * 4 + zh * 2 + core for v in self.ys]
        turn = 2 * (1 - 2 * zh)
        self.zhp = c + turn
        self.yp_z, self.ym_z, self.yo_z = self.yp + turn, self.ym + turn, self.yo + turn
        self.other = 1 - 2 * core
        self.sib = c + self.other

    def on_head(self, index):
        return (index, self.c)

    def on_ctx(self, index):
        return (self.h, index)


def gather_out_grad(me, s):
    def piece(owner, k):
        return s.og.at[owner, pl.ds(k * OG_ROWS, OG_ROWS)]

    def go(kind, owner, to, k):
        ref = piece(owner, k)
        send(ref, ref, s.og_send.at[kind, k], s.og_recv.at[kind, k], me.on_head(to))

    def come(kind, owner, k):
        arrived(piece(owner, k), s.og_recv.at[kind, k], me.on_head(me.zp))

    def gone(kind, owner, k):
        sent(piece(owner, k), s.og_send.at[kind, k], me.on_head(me.zp))

    return go, come, gone


def gather_kv(me, s):
    def piece(owner, k):
        return s.kv.at[pl.ds(owner * ROWS + k * KV_ROWS, KV_ROWS)]

    def go(kind, owner, to, k):
        ref = piece(owner, k)
        send(ref, ref, s.kv_send.at[kind, k], s.kv_recv.at[kind, k], me.on_ctx(to))

    def come(kind, owner, k):
        arrived(piece(owner, k), s.kv_recv.at[kind, k], me.on_ctx(me.sib))

    def gone(kind, owner, k):
        sent(piece(owner, k), s.kv_send.at[kind, k], me.on_ctx(me.sib))

    return go, come, gone


def layer_kernel(n_ctx, index, far, where, q, key, value, out_grad, weight, layer_out, dq, dk, dv, *refs):
    s = Scratch()
    (
        s.qs, s.kvrow, s.sc, s.p, s.ot, s.inv, s.slots, s.att, s.g, s.weight, s.kv, s.table, s.og,
        s.ls, s.lo, s.s1, s.r1, s.s2, s.r2, s.s3, s.r3, w_sem,
        s.og_send, s.og_recv, s.kv_send, s.kv_recv, s.lo_send, s.lo_recv,
        s.send1, s.recv1, s.send2, s.recv2, s.send3, s.recv3, s.send4, s.recv4,
    ) = refs
    s.dq = dq
    me = Place()
    w_copy = pltpu.make_async_copy(weight, s.weight, w_sem)
    w_copy.start()
    mine = pl.multiple_of(me.c * ROWS, ROWS)
    s.kv[pl.ds(mine, ROWS), :, :HD] = key[...]
    s.kv[pl.ds(mine, ROWS), :, HD:] = value[...]
    s.og[me.h] = out_grad[...]

    barrier = pltpu.get_barrier_semaphore()
    partners = [me.on_head(d) for d in (me.xp, me.xm, me.xo, me.zp)]
    partners += [me.on_ctx(d) for d in (me.zhp, me.yp, me.ym, me.yo, me.sib)]
    for device in partners:
        pl.semaphore_signal(barrier, inc=1, device_id=device, device_id_type=MESH)
    pl.semaphore_wait(barrier, len(partners))

    og_go, og_come, og_gone = gather_out_grad(me, s)
    kv_go, kv_come, kv_gone = gather_kv(me, s)
    kv_kinds = [
        (0, me.c, me.yp), (1, me.c, me.ym), (2, me.c, me.yo), (3, me.c, me.zhp),
        (4, me.zhp, me.yp), (5, me.zhp, me.ym), (6, me.yo, me.zhp),
        (7, me.c, me.sib), (8, me.zhp, me.sib), (9, me.ym, me.sib), (10, me.yp, me.sib), (11, me.yo, me.sib),
        (12, me.ym_z, me.sib), (13, me.yp_z, me.sib), (14, me.yo_z, me.sib),
    ]
    og_kinds = {
        0: (0, me.h, me.xp), 1: (1, me.h, me.xm), 3: (3, me.h, me.zp),
        4: (4, me.zp, me.xp), 5: (5, me.zp, me.xm), 6: (6, me.xo, me.zp),
    }

    def kv_start(kinds, k):
        for kind in kinds:
            kv_go(*kv_kinds[kind], k)

    def og_start(kinds, k):
        for kind in kinds:
            og_go(*og_kinds[kind], k)

    def og_across(k):
        og_come(0, me.xm, k)
        og_come(1, me.xp, k)
        og_go(2, me.xm if k % 2 == 0 else me.xp, me.xp if k % 2 == 0 else me.xm, k)

    def og_near(k):
        og_come(3, me.zp, k)
        og_start((4, 5), k)

    def og_far(k):
        og_come(2, me.xo, k)
        og_start((6,), k)

    def kv_pass(k):
        kv_come(3, me.zhp, k)
        kv_start((4, 5, 8), k)

    def kv_near(k):
        for kind, owner in ((0, me.ym), (1, me.yp), (2, me.yo)):
            kv_come(kind, owner, k)
        kv_start((6, 9, 10, 11), k)

    def kv_far(k):
        for kind, owner in ((4, me.ym_z), (5, me.yp_z), (6, me.yo_z)):
            kv_come(kind, owner, k)
        kv_start((12, 13, 14), k)

    def kv_ready(k):
        owners = (me.c, me.zhp, me.ym, me.yp, me.yo, me.ym_z, me.yp_z, me.yo_z)
        for kind, owner in enumerate(owners, 7):
            kv_come(kind, owner + me.other, k)

        @pl.loop(0, n_ctx)
        def _(c):
            at = pl.ds(c * ROWS + k * KV_ROWS, KV_ROWS)
            s.table[at] = s.kv[at]

    for k in range(KV_PARTS):
        kv_start((3,), k)
    for k in range(KV_PARTS):
        kv_start((0, 1, 2, 7), k)
        og_start((0, 1), OG_PARTS - 1 - k)
    og_start((3,), 3)
    og_start((3,), 2)
    s.slots[NOSLOT] = jnp.zeros((BLK, 2 * HD), jnp.bfloat16)
    kv_pass(0)
    og_across(3)
    kv_near(0)
    kv_pass(1)
    og_across(2)
    kv_near(1)
    og_start((3,), 1)
    kv_pass(2)
    kv_pass(3)
    og_across(1)
    kv_near(2)
    og_start((3,), 0)
    og_near(3)
    og_across(0)
    kv_near(3)
    kv_far(0)
    og_near(2)
    kv_ready(0)
    w_copy.wait()

    lo_kinds = [
        (0, me.xo_z, me.zp), (1, me.xp_z, me.xp), (2, me.xm_z, me.xm),
        (3, me.xp, me.xp), (4, me.xm, me.xm), (5, me.xo, None), (6, me.zp, me.zp),
    ]

    def lo_piece(owner, k):
        return s.ls.at[owner, pl.ds(k * OG_ROWS, OG_ROWS)]

    def lo_slot(kind, k):
        return s.lo.at[kind, pl.ds(k * OG_ROWS, OG_ROWS)]

    def lo_start(kind, k):
        _, owner, to = lo_kinds[kind]
        if to is None:
            to = jnp.where(k % 2 == 0, me.xm, me.xp)
        send(lo_piece(owner, k), lo_slot(kind, k), s.lo_send.at[kind, k], s.lo_recv.at[kind, k], me.on_head(to))

    def lo_come(kind, k):
        arrived(lo_slot(kind, k), s.lo_recv.at[kind, k], me.on_head(me.zp))
        return lo_slot(kind, k)[...].astype(jnp.float32)

    def lo_add(owner, k, kinds):
        at = pl.ds(k * OG_ROWS, OG_ROWS)
        total = s.ls[owner, at].astype(jnp.float32)
        for kind in kinds:
            total = total + lo_come(kind, k)
        return total.astype(jnp.bfloat16)

    def share(owner, k):
        cols = pl.ds(pl.multiple_of(owner * NG * HD, NG * HD), NG * HD)
        rows = s.att[pl.ds(k * OG_ROWS, OG_ROWS)].reshape(OG_ROWS * BLK, NG * HD)
        out = dot(rows, s.weight[:, cols], 1, 0).astype(jnp.bfloat16)
        s.ls[owner, pl.ds(k * OG_ROWS, OG_ROWS)] = out.reshape(OG_ROWS, BLK, NG * HD)

    def shares(k):
        for kind in range(5):
            share(lo_kinds[kind][1], k)
            if kind < 3:
                lo_start(kind, k)
        even = k % 2 == 0

        @pl.when(even)
        def _():
            lo_start(3, k)

        @pl.when(jnp.logical_not(even))
        def _():
            lo_start(4, k)

        share(me.xo, k)
        share(me.zp, k)
        share(me.h, k)

    def lo_pass(k):
        at = pl.ds(k * OG_ROWS, OG_ROWS)
        s.ls[me.xo, at] = lo_add(me.xo, k, (0,))
        lo_start(5, k)
        s.ls[me.zp, at] = lo_add(me.zp, k, (1, 2))
        lo_start(6, k)

    def lo_last(k):
        at = pl.ds(k * OG_ROWS, OG_ROWS)
        even = k % 2 == 0
        owner = jnp.where(even, me.xm, me.xp)
        s.ls[owner, at] = lo_add(owner, k, (5,))

        @pl.when(even)
        def _():
            lo_start(4, k)

        @pl.when(jnp.logical_not(even))
        def _():
            lo_start(3, k)

    def lo_final(k):
        layer_out[pl.ds(k * OG_ROWS, OG_ROWS)] = lo_add(me.h, k, (3, 4, 6))

    forward_row(0, 2, index, far, q, s)
    kv_far(1)
    og_near(1)
    og_far(3)
    forward_row(1, 4, index, far, q, s)
    shares(0)

    @pl.loop(1, KV_PARTS)
    def _(k):
        kv_ready(k)

        @pl.loop(0, 2)
        def _(half):
            @pl.when((half == 1) & (k < KV_PARTS - 1))
            def _():
                kv_far(k + 1)

            @pl.when((half == 1) & (k == 1))
            def _():
                og_near(0)

            @pl.when(half == 1)
            def _():
                og_far(KV_PARTS - 1 - k)

            forward_row(2 * k + half, NCH, index, far, q, s)

        shares(k)

    def og_ready(k):
        for kind, owner in ((4, me.xm_z), (5, me.xp_z), (6, me.xo_z)):
            og_come(kind, owner, k)

    def project_grad(k):
        at = pl.ds(k * OG_ROWS, OG_ROWS)
        total = None
        for owner in range(s.og.shape[0]):
            cols = slice(owner * NG * HD, (owner + 1) * NG * HD)
            part = dot(s.og[owner, at].reshape(OG_ROWS * BLK, NG * HD), s.weight[:, cols], 1, 1)
            total = part if total is None else total + part
        s.g[at] = total.astype(jnp.bfloat16).reshape(OG_ROWS, BLK, NG * HD)

    def kv_first(i):
        at = i % HELD

        @pl.when(i < ROWS - HELD)
        def _():
            sent(s.s1.at[at], s.send1.at[i + HELD], me.on_ctx(me.sib))

        @pl.loop(0, n_ctx // 2)
        def _(j):
            u = i * n_ctx + 2 * j + 1 - me.core
            s.s1[at, j] = collect(i, u, where, s).astype(jnp.bfloat16)

        send(s.s1.at[at], s.r1.at[i], s.send1.at[i], s.recv1.at[i], me.on_ctx(me.sib))

        @pl.loop(0, n_ctx // 2)
        def _(j):
            u = i * n_ctx + 2 * j + me.core
            s.s2[i, j] = collect(i, u, where, s).astype(jnp.bfloat16)

    def kv_second(i):
        arrived(s.r1.at[i], s.recv1.at[i], me.on_ctx(me.sib))
        s.s2[i] = (s.s2[i].astype(jnp.float32) + s.r1[i].astype(jnp.float32)).astype(jnp.bfloat16)
        for kind, to in enumerate((me.yp, me.ym)):
            src = s.s2.at[i, pl.ds(2 * me.ys[kind], 2)]
            send(src, s.r2.at[i, kind], s.send2.at[i, kind], s.recv2.at[i, kind], me.on_ctx(to))
        send(far_share(i, 1 - me.zh), s.r2.at[i, 2, 0], s.send4.at[i], s.recv4.at[i], me.on_ctx(me.zhp))

    def far_share(i, zh):
        return s.s2.at[i, 2 * me.ys[2] + zh]

    def kv_far_sum(i):
        arrived(s.r2.at[i, 2, 0], s.recv4.at[i], me.on_ctx(me.zhp))
        ref = far_share(i, me.zh)
        ref[...] = (ref[...].astype(jnp.float32) + s.r2[i, 2, 0].astype(jnp.float32)).astype(jnp.bfloat16)
        send(ref, s.r2.at[i, 2, 1], s.send2.at[i, 2], s.recv2.at[i, 2], me.on_ctx(me.yo))

    def kv_sum(i, zh):
        total = s.s2[i, 2 * me.y + zh].astype(jnp.float32)
        for kind in range(2):
            total = total + s.r2[i, kind, zh].astype(jnp.float32)
        return total

    def kv_third(i):
        kv_far_sum(i)
        for kind in range(2):
            arrived(s.r2.at[i, kind], s.recv2.at[i, kind], me.on_ctx(me.sib))
        s.s3[i] = kv_sum(i, 1 - me.zh).astype(jnp.bfloat16)
        send(s.s3.at[i], s.r3.at[i], s.send3.at[i], s.recv3.at[i], me.on_ctx(me.zhp))

    def kv_final(i):
        arrived(s.r3.at[i], s.recv3.at[i], me.on_ctx(me.sib))
        arrived(s.r2.at[i, 2, 1], s.recv2.at[i, 2], me.on_ctx(me.sib))
        total = kv_sum(i, me.zh) + s.r3[i].astype(jnp.float32) + s.r2[i, 2, 1].astype(jnp.float32)
        dk[i] = (total[:, :HD] * SCALE).astype(jnp.bfloat16)
        dv[i] = total[:, HD:].astype(jnp.bfloat16)

    def step(n, count):
        i = ROWS - 1 - n
        backward_row(i, count, index, s)
        kv_first(i)

        @pl.when(n >= 1)
        def _():
            kv_second(i + 1)

        @pl.when(n >= 3)
        def _():
            kv_third(i + 3)

        @pl.when(n >= 5)
        def _():
            kv_final(i + 5)

    @pl.loop(0, ROWS - 2)
    def _(n):
        @pl.when(n % 2 == 0)
        def _():
            og_ready(OG_PARTS - 1 - n // 2)
            project_grad(OG_PARTS - 1 - n // 2)

        step(n, NCH)

        @pl.when(n < OG_PARTS)
        def _():
            lo_pass(n)

        @pl.when(n >= 2)
        def _():
            lo_last(n - 2)

    og_ready(0)
    project_grad(0)
    step(ROWS - 2, 4)
    step(ROWS - 1, 2)
    kv_second(0)
    kv_third(2)
    lo_final(0)
    lo_final(1)
    kv_third(1)
    kv_final(4)
    kv_final(3)
    lo_final(2)
    kv_third(0)
    kv_final(2)
    kv_final(1)
    lo_final(3)
    kv_final(0)

    @pl.loop(0, OG_PARTS)
    def _(k):
        for kind, owner, to in og_kinds.values():
            og_gone(kind, owner, k)
        og_gone(2, me.xm, k)
        for kind, owner, to in lo_kinds:
            sent(lo_piece(owner, k), s.lo_send.at[kind, k], me.on_head(me.zp))

    @pl.loop(0, KV_PARTS)
    def _(k):
        for kind, owner, to in kv_kinds:
            kv_gone(kind, owner, k)

    @pl.loop(0, ROWS)
    def _(i):
        for kind in range(2):
            sent(s.s2.at[i, pl.ds(0, 2)], s.send2.at[i, kind], me.on_ctx(me.sib))
        sent(s.s2.at[i, 0], s.send2.at[i, 2], me.on_ctx(me.sib))
        sent(s.s2.at[i, 0], s.send4.at[i], me.on_ctx(me.sib))
        sent(s.s3.at[i], s.send3.at[i], me.on_ctx(me.zhp))

    @pl.loop(0, HELD)
    def _(i):
        sent(s.s1.at[i], s.send1.at[i], me.on_ctx(me.sib))


def hand_over_kernel(*refs):
    count = len(refs) // 2
    for k in range(count):
        refs[count + k][...] = refs[k][...]


def hand_over(arrays):
    vmem = pl.BlockSpec(memory_space=pltpu.VMEM)
    return pl.pallas_call(
        hand_over_kernel,
        out_shape=[jax.ShapeDtypeStruct(x.shape, x.dtype) for x in arrays],
        in_specs=[vmem] * len(arrays),
        out_specs=[vmem] * len(arrays),
        name="hand_over",
    )(*arrays)


def layer(index, far, where, q, key, value, out_grad, weight, n_head, n_ctx):
    smem = pl.BlockSpec(memory_space=pltpu.SMEM)
    vmem = pl.BlockSpec(memory_space=pltpu.VMEM)
    wide, narrow = (ROWS, BLK, NG * HD), (ROWS, BLK, HD)
    low = jnp.bfloat16
    sem = pltpu.SemaphoreType.DMA
    return pl.pallas_call(
        functools.partial(layer_kernel, n_ctx),
        out_shape=[jax.ShapeDtypeStruct(shape, low) for shape in (wide, wide, narrow, narrow)],
        in_specs=[smem] * 3 + [vmem] * 4 + [pl.BlockSpec(memory_space=pl.ANY)],
        out_specs=[vmem] * 4,
        scratch_shapes=[
            pltpu.VMEM((ROWS, QN, HD), low),
            pltpu.VMEM((NCH, CK, 2 * HD), low),
            pltpu.VMEM((NCH, CK, QN), jnp.float32),
            pltpu.VMEM((CHUNKS, CK, QN), low),
            pltpu.VMEM((ROWS, HD, QN), low),
            pltpu.VMEM((ROWS, 8, QN), jnp.float32),
            pltpu.VMEM((NOSLOT + 1, BLK, 2 * HD), low),
            pltpu.VMEM(wide, low),
            pltpu.VMEM(wide, low),
            pltpu.VMEM(weight.shape, low),
            pltpu.VMEM((n_ctx * ROWS, BLK, 2 * HD), low),
            pltpu.VMEM((n_ctx * ROWS, BLK, 2 * HD), low),
            pltpu.VMEM((n_head,) + wide, low),
            pltpu.VMEM((n_head,) + wide, low),
            pltpu.VMEM((7,) + wide, low),
            pltpu.VMEM((HELD, n_ctx // 2, BLK, 2 * HD), low),
            pltpu.VMEM((ROWS, n_ctx // 2, BLK, 2 * HD), low),
            pltpu.VMEM((ROWS, n_ctx // 2, BLK, 2 * HD), low),
            pltpu.VMEM((ROWS, 3, 2, BLK, 2 * HD), low),
            pltpu.VMEM((ROWS, BLK, 2 * HD), low),
            pltpu.VMEM((ROWS, BLK, 2 * HD), low),
            sem,
            sem((7, OG_PARTS)), sem((7, OG_PARTS)),
            sem((15, KV_PARTS)), sem((15, KV_PARTS)),
            sem((7, OG_PARTS)), sem((7, OG_PARTS)),
            sem((ROWS,)), sem((ROWS,)),
            sem((ROWS, 3)), sem((ROWS, 3)),
            sem((ROWS,)), sem((ROWS,)),
            sem((ROWS,)), sem((ROWS,)),
        ],
        compiler_params=pltpu.CompilerParams(
            vmem_limit_bytes=63 << 20, collective_id=0, has_side_effects=True
        ),
        name="layer",
    )(index, far, where, q, key, value, out_grad, weight)


def on_device(query, key, value, out_grad, weight, vertical, slash):
    n_head, n_ctx = lax.axis_size("head"), lax.axis_size("ctx")
    index, far, where = lists(vertical[0, :, 0], slash[0, :, 0], lax.axis_index("ctx"), n_ctx)
    outs = layer(
        index, far, where, query[:, 0], key[:, 0], value[:, 0], out_grad[:, 0], weight, n_head, n_ctx
    )
    return tuple(x[:, None] for x in hand_over(outs))


def solution(mesh):
    spread = P(None, "ctx", None, "head")
    listed = P("head", None, "ctx", None)
    return jax.shard_map(
        on_device,
        mesh=mesh,
        in_specs=(spread, spread, spread, spread, P("head", None), listed, listed),
        out_specs=(spread,) * 4,
        check_vma=False,
    )
```

time: 125 us -> 98.4 us (0.79)
  Pallas kernels: 112 us -> 91.8 us
  local copies, waits for them, and re-layouts: 6.87 us -> 0 us
    pallas_call x1, Pallas kernels: 112 us -> 89.4 us  [layer(): pl.pallas_call(functools.partial(layer_kernel, n_ctx), out_shape=[jax.Sha...]
    unnamed x4 -> x0, local copies, waits for them, and re-layouts: 6.87 us -> none
    pallas_call x0 -> x1, Pallas kernels: none -> 2.34 us  [hand_over(): pl.pallas_call(hand_over_kernel, out_shape=[jax.ShapeDtypeStruct(x.shape,...]
where the time goes in v2:
time: 98.4 us; the launch traced here: 96.7 us
  Pallas kernels  91.8 us (93%)
  other arithmetic  4.26 us (4%)
    pallas_call x1, Pallas kernels, layer(): pl.pallas_call(functools.partial(layer_kernel, n_ctx), out_shape=[jax.Sha...  89.4 us
    pallas_call x1, Pallas kernels, hand_over(): pl.pallas_call(hand_over_kernel, out_shape=[jax.ShapeDtypeStruct(x.shape,...  2.34 us

profile of v2, /device:TPU:2, one launch (start us, length us, event | category | flops | bytes accessed | tf_op | source)
XLA Modules:
  0.0 96.7 jit_solution(8976985751608112595)
XLA Ops:
  0.7 0.8 broadcast_subtract_fusion
  1.4 0.8 compare_and_fusion
  2.2 0.2 convert_reduce_fusion
  2.4 0.1 add_add_fusion
  2.5 0.2 select_reduce_fusion
  2.7 0.6 broadcast_add_fusion.where
  3.3 0.2 fusion
  3.5 0.8 select_reduce_fusion.1.index
  4.3 0.6 broadcast_select_fusion.far
  4.9 89.4 %layer.1 = (bf16[8,64,512]{2,1,0:T(8,128)(2,1)}, bf16[8,64,512]{2,1,0:T(8,128)(2,1)}, bf16[8,64,128]{2,1,0:T(8,128)(2,1)}, bf16[8,64,128]{2,1,0:T(8,128)(2,1)}) custom-call(s32[8,40]{1,0:T(8,128)} %select_reduce_fusion.1.index, f32[8,40]{1,0:T(8,128)} %broadcast_select_fusion.far, s32[8,128]{1,0:T(8,128)} %broadcast_add_fusion.where, ...), custom_call_target="tpu_custom_call" | custom-call | tf_op jit(solution)/shard_map/layer/pallas_call | solution.py:603
  94.4 2.3 %hand_over.1 = (bf16[8,64,512]{2,1,0:T(8,128)(2,1)}, bf16[8,64,512]{2,1,0:T(8,128)(2,1)}, bf16[8,64,128]{2,1,0:T(8,128)(2,1)}, bf16[8,64,128]{2,1,0:T(8,128)(2,1)}) custom-call(bf16[8,64,512]{2,1,0:T(8,128)(2,1)} %get-tuple-element.12.refs_0_, bf16[8,64,512]{2,1,0:T(8,128)(2,1)} %get-tuple-element.13.refs_1_, bf16[8,64,128]{2,1,0:T(8,128)(2,1)} %get-tuple-element.14.refs_2_, ...), custom_call_target="tpu_custom_call" | custom-call | tf_op jit(solution)/shard_map/hand_over/pallas_call | solution.py:588
  (3 shorter events, 0.0 us)

commit v3 on v2

--- a/solution.py
+++ b/solution.py
@@ -36,15 +36,19 @@
     order = jnp.arange(NE, dtype=jnp.int32)
     place = jnp.sum((kept[:, None, :] & (order[None, None, :] < order[None, :, None])).astype(jnp.int32), axis=2)
     place = jnp.where(kept, place, NE)
-    here = place[:, None, :] == order[None, :, None]
     moved = raw % n_ctx * ROWS + raw // n_ctx
-    index = jnp.sum(jnp.where(here, moved[:, None, :], 0), axis=2)
-    far = jnp.where(jnp.any(here, axis=2), 0.0, FAR).astype(jnp.float32)
     slot = chunk_base(rows)[:, None] * EPC + place
-    block = jnp.arange(ROWS * n_ctx, dtype=jnp.int32)
-    hit = (raw[:, None, :] == block[None, :, None]) & kept[:, None, :]
-    where = NOSLOT + jnp.sum(jnp.where(hit, slot[:, None, :] - NOSLOT, 0), axis=2)
-    return index, far, where
+    blocks = ROWS * n_ctx
+    column = jnp.arange(NE + blocks + 1, dtype=jnp.int32)[None, :, None]
+    by_place = place[:, None, :] == column
+    by_block = kept[:, None, :] & (raw[:, None, :] == column - NE)
+    last = column == NE + blocks
+    picked = jnp.where(by_place & (column < NE), moved[:, None, :], 0)
+    picked = jnp.where(by_block, slot[:, None, :] - NOSLOT, picked)
+    picked = jnp.where(last, kept[:, None, :].astype(jnp.int32), picked)
+    table = jnp.sum(picked, axis=2)
+    block_column = (column[..., 0] >= NE) & (column[..., 0] < NE + blocks)
+    return jnp.where(block_column, table + NOSLOT, table)
 
 
 def dot(a, b, ca, cb):
@@ -59,13 +63,18 @@
     return jnp.concatenate([x[h * BLK:(h + 1) * BLK] for h in range(NG)], axis=1)
 
 
-def forward_row(i, count, index, far, q, s):
+def forward_row(i, count, index, q, s):
     qs = heads_down(q[i])
     s.qs[i] = qs
     base = chunk_base(i)
     key_pos = lax.broadcasted_iota(jnp.int32, (BLK, QN), 0)
     query_pos = lax.broadcasted_iota(jnp.int32, (BLK, QN), 1) % BLK
     top = jnp.full((8, QN), FAR, jnp.float32)
+    entries = index[i, index.shape[1] - 1]
+
+    def far(at):
+        return jnp.where(at < entries, 0.0, FAR)
+
     for ch in range(count):
         for e in range(EPC):
             s.kvrow[ch, e * BLK:(e + 1) * BLK, :] = s.table[index[i, ch * EPC + e]]
@@ -76,14 +85,14 @@
                 part = jnp.where(key_pos <= query_pos, part, FAR)
             s.sc[ch, e * BLK:(e + 1) * BLK, :] = part
             part = jnp.max(part.reshape(BLK // 8, 8, QN), axis=0)
-            top = jnp.maximum(top, part + far[i, ch * EPC + e])
+            top = jnp.maximum(top, part + far(ch * EPC + e))
     top = jnp.max(top, axis=0, keepdims=True) * (SCALE * LOG2E)
 
     total = jnp.zeros((8, QN), jnp.float32)
     acc = jnp.zeros((HD, QN), jnp.float32)
     for ch in range(count):
         for e in range(EPC):
-            shift = top - far[i, ch * EPC + e]
+            shift = top - far(ch * EPC + e)
             p = jnp.exp2(s.sc[ch, e * BLK:(e + 1) * BLK, :] * (SCALE * LOG2E) - shift)
             total = total + jnp.sum(p.reshape(BLK // 8, 8, QN), axis=0)
             s.p[base + ch, e * BLK:(e + 1) * BLK, :] = p.astype(jnp.bfloat16)
@@ -103,25 +112,43 @@
     delta = jnp.sum(g32 * s.ot[i].astype(jnp.float32), axis=0, keepdims=True)
     gs = g32.T.astype(jnp.bfloat16)
     qs = s.qs[i]
-    acc = jnp.zeros((HD, QN), jnp.float32)
     for ch in range(count):
         for e in range(EPC):
-            s.kvrow[ch, e * BLK:(e + 1) * BLK, :] = s.table[index[i, ch * EPC + e]]
+            s.kvrow[ch, e * BLK:(e + 1) * BLK, HD:] = s.table[index[i, ch * EPC + e], :, HD:]
         dp = dot(s.kvrow[ch, :, HD:], gt, 1, 0)
         p = s.p[base + ch]
         ds = (p.astype(jnp.float32) * (dp - delta)).astype(jnp.bfloat16)
         at = pl.ds((base + ch) * EPC, EPC)
         s.slots[at, :, :HD] = dot(ds, qs, 1, 0).astype(jnp.bfloat16).reshape(EPC, BLK, HD)
         s.slots[at, :, HD:] = dot(p, gs, 1, 0).astype(jnp.bfloat16).reshape(EPC, BLK, HD)
-        acc = acc + dot(s.kvrow[ch, :, :HD], ds, 0, 0)
+        s.p[base + ch] = ds
+
+
+def query_row(i, count, index, s):
+    acc = jnp.zeros((HD, QN), jnp.float32)
+    base = chunk_base(i)
+    for ch in range(count):
+        for e in range(EPC):
+            s.kvrow[ch, e * BLK:(e + 1) * BLK, :HD] = s.table[index[i, ch * EPC + e], :, :HD]
+        acc = acc + dot(s.kvrow[ch, :, :HD], s.p[base + ch], 0, 0)
     s.dq[i] = heads_across((acc * SCALE).T).astype(jnp.bfloat16)
 
 
-def collect(i, u, where, s):
-    def more(r, acc):
-        return acc + s.slots[where[r, u]].astype(jnp.float32)
-
-    return lax.fori_loop(i, ROWS, more, jnp.zeros((BLK, 2 * HD), jnp.float32))
+def collect(first, u, index, s):
+    total = s.slots[index[first, NE + u]].astype(jnp.float32)
+    for r in range(first + 1, ROWS):
+        total = total + s.slots[index[r, NE + u]].astype(jnp.float32)
+    return total
+
+
+def collect_row(i, core, n_ctx, index, s, out):
+    for first in range(ROWS):
+
+        @pl.when(i == first)
+        def _():
+            @pl.loop(0, n_ctx // 2)
+            def _(j):
+                out[j] = collect(first, first * n_ctx + 2 * j + core, index, s).astype(jnp.bfloat16)
 
 
 class Scratch:
@@ -133,6 +160,7 @@
 OG_ROWS = ROWS // OG_PARTS
 HELD = 4
 KV_PARTS = 4
+OVER_Y = 2
 KV_ROWS = ROWS // KV_PARTS
 
 
@@ -214,13 +242,13 @@
     return go, come, gone
 
 
-def layer_kernel(n_ctx, index, far, where, q, key, value, out_grad, weight, layer_out, dq, dk, dv, *refs):
+def layer_kernel(n_ctx, index, q, key, value, out_grad, weight, layer_out, dq, dk, dv, *refs):
     s = Scratch()
     (
-        s.qs, s.kvrow, s.sc, s.p, s.ot, s.inv, s.slots, s.att, s.g, s.weight, s.kv, s.table, s.og,
+        s.qs, s.kvrow, s.sc, s.p, s.ot, s.inv, s.slots, s.att, s.g, s.acc, s.weight, s.kv, s.table, s.og,
         s.ls, s.lo, s.s1, s.r1, s.s2, s.r2, s.s3, s.r3, w_sem,
         s.og_send, s.og_recv, s.kv_send, s.kv_recv, s.lo_send, s.lo_recv,
-        s.send1, s.recv1, s.send2, s.recv2, s.send3, s.recv3, s.send4, s.recv4,
+        s.send1, s.recv1, s.send2, s.recv2, s.send3, s.recv3, s.send4, s.recv4, s.send5, s.recv5,
     ) = refs
     s.dq = dq
     me = Place()
@@ -233,7 +261,8 @@
 
     barrier = pltpu.get_barrier_semaphore()
     partners = [me.on_head(d) for d in (me.xp, me.xm, me.xo, me.zp)]
-    partners += [me.on_ctx(d) for d in (me.zhp, me.yp, me.ym, me.yo, me.sib)]
+    column = (me.yp, me.ym, me.yo, me.yp_z, me.ym_z, me.yo_z, me.zhp)
+    partners += [me.on_ctx(d) for d in column + (me.sib,)]
     for device in partners:
         pl.semaphore_signal(barrier, inc=1, device_id=device, device_id_type=MESH)
     pl.semaphore_wait(barrier, len(partners))
@@ -242,7 +271,7 @@
     kv_go, kv_come, kv_gone = gather_kv(me, s)
     kv_kinds = [
         (0, me.c, me.yp), (1, me.c, me.ym), (2, me.c, me.yo), (3, me.c, me.zhp),
-        (4, me.zhp, me.yp), (5, me.zhp, me.ym), (6, me.yo, me.zhp),
+        (4, me.zhp, me.yp), (5, me.zhp, me.ym), (6, me.zhp, me.yo),
         (7, me.c, me.sib), (8, me.zhp, me.sib), (9, me.ym, me.sib), (10, me.yp, me.sib), (11, me.yo, me.sib),
         (12, me.ym_z, me.sib), (13, me.yp_z, me.sib), (14, me.yo_z, me.sib),
     ]
@@ -272,14 +301,24 @@
         og_come(2, me.xo, k)
         og_start((6,), k)
 
+    def project_early(owner, first):
+        cols = pl.ds(pl.multiple_of(owner * NG * HD, NG * HD), NG * HD)
+        part = dot(s.og[owner].reshape(ROWS * BLK, NG * HD), s.weight[:, cols], 1, 1)
+        part = part.reshape(ROWS, BLK, NG * HD)
+        s.acc[...] = part if first else s.acc[...] + part
+
     def kv_pass(k):
         kv_come(3, me.zhp, k)
+        if k < OVER_Y:
+            kv_start((6,), k)
         kv_start((4, 5, 8), k)
 
     def kv_near(k):
         for kind, owner in ((0, me.ym), (1, me.yp), (2, me.yo)):
             kv_come(kind, owner, k)
-        kv_start((6, 9, 10, 11), k)
+        if k >= OVER_Y:
+            kv_go(6, me.yo, me.zhp, k)
+        kv_start((9, 10, 11), k)
 
     def kv_far(k):
         for kind, owner in ((4, me.ym_z), (5, me.yp_z), (6, me.yo_z)):
@@ -298,31 +337,35 @@
 
     for k in range(KV_PARTS):
         kv_start((3,), k)
-    for k in range(KV_PARTS):
-        kv_start((0, 1, 2, 7), k)
+    for k in range(2):
+        kv_start((2, 0, 1, 7), k)
         og_start((0, 1), OG_PARTS - 1 - k)
     og_start((3,), 3)
     og_start((3,), 2)
+    og_start((0, 1), 1)
+    og_start((0, 1), 0)
     s.slots[NOSLOT] = jnp.zeros((BLK, 2 * HD), jnp.bfloat16)
     kv_pass(0)
+    kv_start((2, 0, 1, 7), 2)
     og_across(3)
+    kv_pass(1)
+    kv_start((2, 0, 1, 7), 3)
     kv_near(0)
-    kv_pass(1)
+    kv_pass(2)
     og_across(2)
+    kv_pass(3)
+    og_start((3,), 1)
+    og_start((3,), 0)
     kv_near(1)
-    og_start((3,), 1)
-    kv_pass(2)
-    kv_pass(3)
     og_across(1)
-    kv_near(2)
-    og_start((3,), 0)
     og_near(3)
+    kv_far(0)
     og_across(0)
-    kv_near(3)
-    kv_far(0)
     og_near(2)
+    w_copy.wait()
+    for owner in (me.h, me.xm, me.xp):
+        project_early(owner, owner is me.h)
     kv_ready(0)
-    w_copy.wait()
 
     lo_kinds = [
         (0, me.xo_z, me.zp), (1, me.xp_z, me.xp), (2, me.xm_z, me.xm),
@@ -401,11 +444,12 @@
     def lo_final(k):
         layer_out[pl.ds(k * OG_ROWS, OG_ROWS)] = lo_add(me.h, k, (3, 4, 6))
 
-    forward_row(0, 2, index, far, q, s)
+    forward_row(0, 2, index, q, s)
+    kv_near(2)
+    forward_row(1, 4, index, q, s)
+    og_far(3)
     kv_far(1)
     og_near(1)
-    og_far(3)
-    forward_row(1, 4, index, far, q, s)
     shares(0)
 
     @pl.loop(1, KV_PARTS)
@@ -414,19 +458,20 @@
 
         @pl.loop(0, 2)
         def _(half):
+            @pl.when((half == 1) & (k == 1))
+            def _():
+                kv_near(3)
+                og_near(0)
+
             @pl.when((half == 1) & (k < KV_PARTS - 1))
             def _():
                 kv_far(k + 1)
 
-            @pl.when((half == 1) & (k == 1))
-            def _():
-                og_near(0)
-
             @pl.when(half == 1)
             def _():
                 og_far(KV_PARTS - 1 - k)
 
-            forward_row(2 * k + half, NCH, index, far, q, s)
+            forward_row(2 * k + half, NCH, index, q, s)
 
         shares(k)
 
@@ -436,11 +481,11 @@
 
     def project_grad(k):
         at = pl.ds(k * OG_ROWS, OG_ROWS)
-        total = None
-        for owner in range(s.og.shape[0]):
-            cols = slice(owner * NG * HD, (owner + 1) * NG * HD)
-            part = dot(s.og[owner, at].reshape(OG_ROWS * BLK, NG * HD), s.weight[:, cols], 1, 1)
-            total = part if total is None else total + part
+        total = s.acc[at].reshape(OG_ROWS * BLK, NG * HD)
+        for owner in (me.zp, me.xo, me.xm_z, me.xp_z, me.xo_z):
+            cols = pl.ds(pl.multiple_of(owner * NG * HD, NG * HD), NG * HD)
+            rows = s.og[owner, at].reshape(OG_ROWS * BLK, NG * HD)
+            total = total + dot(rows, s.weight[:, cols], 1, 1)
         s.g[at] = total.astype(jnp.bfloat16).reshape(OG_ROWS, BLK, NG * HD)
 
     def kv_first(i):
@@ -450,17 +495,9 @@
         def _():
             sent(s.s1.at[at], s.send1.at[i + HELD], me.on_ctx(me.sib))
 
-        @pl.loop(0, n_ctx // 2)
-        def _(j):
-            u = i * n_ctx + 2 * j + 1 - me.core
-            s.s1[at, j] = collect(i, u, where, s).astype(jnp.bfloat16)
-
+        collect_row(i, 1 - me.core, n_ctx, index, s, s.s1.at[at])
         send(s.s1.at[at], s.r1.at[i], s.send1.at[i], s.recv1.at[i], me.on_ctx(me.sib))
-
-        @pl.loop(0, n_ctx // 2)
-        def _(j):
-            u = i * n_ctx + 2 * j + me.core
-            s.s2[i, j] = collect(i, u, where, s).astype(jnp.bfloat16)
+        collect_row(i, me.core, n_ctx, index, s, s.s2.at[i])
 
     def kv_second(i):
         arrived(s.r1.at[i], s.recv1.at[i], me.on_ctx(me.sib))
@@ -470,6 +507,26 @@
             send(src, s.r2.at[i, kind], s.send2.at[i, kind], s.recv2.at[i, kind], me.on_ctx(to))
         send(far_share(i, 1 - me.zh), s.r2.at[i, 2, 0], s.send4.at[i], s.recv4.at[i], me.on_ctx(me.zhp))
 
+    def kv_direct():
+        arrived(s.r1.at[0], s.recv1.at[0], me.on_ctx(me.sib))
+        s.s2[0] = (s.s2[0].astype(jnp.float32) + s.r1[0].astype(jnp.float32)).astype(jnp.bfloat16)
+        for k, to in enumerate(column):
+            send(s.s2.at[0, to // 2], direct_slot(k), s.send5.at[k], s.recv5.at[k], me.on_ctx(to))
+
+    def direct_slot(k):
+        return s.r2.at[0, k // 2, k % 2] if k < 6 else s.r3.at[0]
+
+    def kv_direct_final():
+        total = s.s2[0, me.c // 2].astype(jnp.float32)
+        for k in range(7):
+            arrived(direct_slot(k), s.recv5.at[k], me.on_ctx(me.sib))
+            total = total + direct_slot(k)[...].astype(jnp.float32)
+        kv_write(0, total)
+
+    def kv_write(i, total):
+        dk[i] = (total[:, :HD] * SCALE).astype(jnp.bfloat16)
+        dv[i] = total[:, HD:].astype(jnp.bfloat16)
+
     def far_share(i, zh):
         return s.s2.at[i, 2 * me.ys[2] + zh]
 
@@ -496,8 +553,7 @@
         arrived(s.r3.at[i], s.recv3.at[i], me.on_ctx(me.sib))
         arrived(s.r2.at[i, 2, 1], s.recv2.at[i, 2], me.on_ctx(me.sib))
         total = kv_sum(i, me.zh) + s.r3[i].astype(jnp.float32) + s.r2[i, 2, 1].astype(jnp.float32)
-        dk[i] = (total[:, :HD] * SCALE).astype(jnp.bfloat16)
-        dv[i] = total[:, HD:].astype(jnp.bfloat16)
+        kv_write(i, total)
 
     def step(n, count):
         i = ROWS - 1 - n
@@ -525,31 +581,41 @@
 
         step(n, NCH)
 
-        @pl.when(n < OG_PARTS)
-        def _():
-            lo_pass(n)
-
-        @pl.when(n >= 2)
-        def _():
-            lo_last(n - 2)
+        @pl.when((n >= 1) & (n < 1 + OG_PARTS))
+        def _():
+            lo_pass(n - 1)
+
+        @pl.when(n >= 3)
+        def _():
+            lo_last(n - 3)
 
     og_ready(0)
     project_grad(0)
     step(ROWS - 2, 4)
+    lo_last(3)
     step(ROWS - 1, 2)
-    kv_second(0)
+    def query_rows(low):
+        @pl.loop(low, low + 2)
+        def _(i):
+            query_row(i, NCH, index, s)
+
+    query_rows(6)
+    kv_direct()
     kv_third(2)
+    query_rows(4)
+    kv_third(1)
     lo_final(0)
     lo_final(1)
-    kv_third(1)
+    query_rows(2)
     kv_final(4)
     kv_final(3)
+    kv_final(1)
+    kv_final(2)
+    query_row(1, 4, index, s)
+    query_row(0, 2, index, s)
     lo_final(2)
-    kv_third(0)
-    kv_final(2)
-    kv_final(1)
     lo_final(3)
-    kv_final(0)
+    kv_direct_final()
 
     @pl.loop(0, OG_PARTS)
     def _(k):
@@ -564,7 +630,10 @@
         for kind, owner, to in kv_kinds:
             kv_gone(kind, owner, k)
 
-    @pl.loop(0, ROWS)
+    for k in range(7):
+        sent(s.s2.at[0, 0], s.send5.at[k], me.on_ctx(me.sib))
+
+    @pl.loop(1, ROWS)
     def _(i):
         for kind in range(2):
             sent(s.s2.at[i, pl.ds(0, 2)], s.send2.at[i, kind], me.on_ctx(me.sib))
@@ -594,7 +663,7 @@
     )(*arrays)
 
 
-def layer(index, far, where, q, key, value, out_grad, weight, n_head, n_ctx):
+def layer(index, q, key, value, out_grad, weight, n_head, n_ctx):
     smem = pl.BlockSpec(memory_space=pltpu.SMEM)
     vmem = pl.BlockSpec(memory_space=pltpu.VMEM)
     wide, narrow = (ROWS, BLK, NG * HD), (ROWS, BLK, HD)
@@ -603,7 +672,7 @@
     return pl.pallas_call(
         functools.partial(layer_kernel, n_ctx),
         out_shape=[jax.ShapeDtypeStruct(shape, low) for shape in (wide, wide, narrow, narrow)],
-        in_specs=[smem] * 3 + [vmem] * 4 + [pl.BlockSpec(memory_space=pl.ANY)],
+        in_specs=[smem] + [vmem] * 4 + [pl.BlockSpec(memory_space=pl.ANY)],
         out_specs=[vmem] * 4,
         scratch_shapes=[
             pltpu.VMEM((ROWS, QN, HD), low),
@@ -615,6 +684,7 @@
             pltpu.VMEM((NOSLOT + 1, BLK, 2 * HD), low),
             pltpu.VMEM(wide, low),
             pltpu.VMEM(wide, low),
+            pltpu.VMEM(wide, jnp.float32),
             pltpu.VMEM(weight.shape, low),
             pltpu.VMEM((n_ctx * ROWS, BLK, 2 * HD), low),
             pltpu.VMEM((n_ctx * ROWS, BLK, 2 * HD), low),
@@ -635,19 +705,20 @@
             sem((ROWS, 3)), sem((ROWS, 3)),
             sem((ROWS,)), sem((ROWS,)),
             sem((ROWS,)), sem((ROWS,)),
+            sem((7,)), sem((7,)),
         ],
         compiler_params=pltpu.CompilerParams(
             vmem_limit_bytes=63 << 20, collective_id=0, has_side_effects=True
         ),
         name="layer",
-    )(index, far, where, q, key, value, out_grad, weight)
+    )(index, q, key, value, out_grad, weight)
 
 
 def on_device(query, key, value, out_grad, weight, vertical, slash):
     n_head, n_ctx = lax.axis_size("head"), lax.axis_size("ctx")
-    index, far, where = lists(vertical[0, :, 0], slash[0, :, 0], lax.axis_index("ctx"), n_ctx)
+    index = lists(vertical[0, :, 0], slash[0, :, 0], lax.axis_index("ctx"), n_ctx)
     outs = layer(
-        index, far, where, query[:, 0], key[:, 0], value[:, 0], out_grad[:, 0], weight, n_head, n_ctx
+        index, query[:, 0], key[:, 0], value[:, 0], out_grad[:, 0], weight, n_head, n_ctx
     )
     return tuple(x[:, None] for x in hand_over(outs))
 

time: 98.4 us -> 89.3 us (0.908); the launches traced: 96.7 us -> 89.1 us
  Pallas kernels: 91.8 us -> 85.6 us
  other arithmetic: 4.26 us -> 2.79 us
    pallas_call x1, Pallas kernels: 89.4 us -> 83.3 us  [layer(): pl.pallas_call(functools.partial(layer_kernel, n_ctx), out_shape=[jax.Sha...]
where the time goes in v3:
time: 89.3 us; the launch traced here: 89.1 us
  Pallas kernels  85.6 us (96%)
  other arithmetic  2.79 us (3%)
    pallas_call x1, Pallas kernels, layer(): pl.pallas_call(functools.partial(layer_kernel, n_ctx), out_shape=[jax.Sha...  83.3 us
    pallas_call x1, Pallas kernels, hand_over(): pl.pallas_call(hand_over_kernel, out_shape=[jax.ShapeDtypeStruct(x.shape,...  2.34 us

profile of v3, /device:TPU:2, one launch (start us, length us, event | category | flops | bytes accessed | tf_op | source)
XLA Modules:
  0.0 89.1 jit_solution(257785135126062374)
XLA Ops:
  0.7 0.8 broadcast_subtract_fusion
  1.5 0.8 fusion.9
  2.2 0.2 convert_reduce_fusion
  2.5 0.1 add_add_fusion
  2.5 0.3 select_reduce_fusion
  2.9 0.6 add_select_fusion.index
  3.5 83.3 %layer.1 = (bf16[8,64,512]{2,1,0:T(8,128)(2,1)}, bf16[8,64,512]{2,1,0:T(8,128)(2,1)}, bf16[8,64,128]{2,1,0:T(8,128)(2,1)}, bf16[8,64,128]{2,1,0:T(8,128)(2,1)}) custom-call(s32[8,169]{1,0:T(8,128)} %add_select_fusion.index, bf16[8,64,512]{2,1,0:T(8,128)(2,1)} %bitcast.18, bf16[8,64,128]{2,1,0:T(8,128)(2,1)} %bitcast.20, bf16[8,64,128]{2,1,0:T(8,128)(2,1)} %bitcast.21, ...), custom_call_target="tpu_custom_call" | custom-call | tf_op jit(solution)/shard_map/layer/pallas_call | solution.py:672
  86.8 2.3 %hand_over.1 = (bf16[8,64,512]{2,1,0:T(8,128)(2,1)}, bf16[8,64,512]{2,1,0:T(8,128)(2,1)}, bf16[8,64,128]{2,1,0:T(8,128)(2,1)}, bf16[8,64,128]{2,1,0:T(8,128)(2,1)}) custom-call(bf16[8,64,512]{2,1,0:T(8,128)(2,1)} %get-tuple-element.12.refs_0_, bf16[8,64,512]{2,1,0:T(8,128)(2,1)} %get-tuple-element.13.refs_1_, bf16[8,64,128]{2,1,0:T(8,128)(2,1)} %get-tuple-element.14.refs_2_, ...), custom_call_target="tpu_custom_call" | custom-call | tf_op jit(solution)/shard_map/hand_over/pallas_call | solution.py:657
  (6 shorter events, 0.0 us)

commit v4 on v3

--- a/solution.py
+++ b/solution.py
@@ -18,7 +18,8 @@
 NCH = NE // EPC
 QN = NG * BLK
 CHUNKS = 36
-NOSLOT = CHUNKS * EPC
+NOSLOT = 0
+FIRST = 1
 SCALE = 1.0 / math.sqrt(HD)
 LOG2E = 1.4426950408889634
 FAR = -1e30
@@ -37,18 +38,16 @@
     place = jnp.sum((kept[:, None, :] & (order[None, None, :] < order[None, :, None])).astype(jnp.int32), axis=2)
     place = jnp.where(kept, place, NE)
     moved = raw % n_ctx * ROWS + raw // n_ctx
-    slot = chunk_base(rows)[:, None] * EPC + place
+    slot = FIRST + chunk_base(rows)[:, None] * EPC + place
     blocks = ROWS * n_ctx
     column = jnp.arange(NE + blocks + 1, dtype=jnp.int32)[None, :, None]
     by_place = place[:, None, :] == column
     by_block = kept[:, None, :] & (raw[:, None, :] == column - NE)
     last = column == NE + blocks
     picked = jnp.where(by_place & (column < NE), moved[:, None, :], 0)
-    picked = jnp.where(by_block, slot[:, None, :] - NOSLOT, picked)
+    picked = jnp.where(by_block, slot[:, None, :], picked)
     picked = jnp.where(last, kept[:, None, :].astype(jnp.int32), picked)
-    table = jnp.sum(picked, axis=2)
-    block_column = (column[..., 0] >= NE) & (column[..., 0] < NE + blocks)
-    return jnp.where(block_column, table + NOSLOT, table)
+    return jnp.sum(picked, axis=2)
 
 
 def dot(a, b, ca, cb):
@@ -118,7 +117,7 @@
         dp = dot(s.kvrow[ch, :, HD:], gt, 1, 0)
         p = s.p[base + ch]
         ds = (p.astype(jnp.float32) * (dp - delta)).astype(jnp.bfloat16)
-        at = pl.ds((base + ch) * EPC, EPC)
+        at = pl.ds(FIRST + (base + ch) * EPC, EPC)
         s.slots[at, :, :HD] = dot(ds, qs, 1, 0).astype(jnp.bfloat16).reshape(EPC, BLK, HD)
         s.slots[at, :, HD:] = dot(p, gs, 1, 0).astype(jnp.bfloat16).reshape(EPC, BLK, HD)
         s.p[base + ch] = ds
@@ -242,11 +241,11 @@
     return go, come, gone
 
 
-def layer_kernel(n_ctx, index, q, key, value, out_grad, weight, layer_out, dq, dk, dv, *refs):
+def layer_kernel(n_ctx, index, query, key, value, out_grad, weight, layer_out, dq, dk, dv, *refs):
     s = Scratch()
     (
-        s.qs, s.kvrow, s.sc, s.p, s.ot, s.inv, s.slots, s.att, s.g, s.acc, s.weight, s.kv, s.table, s.og,
-        s.ls, s.lo, s.s1, s.r1, s.s2, s.r2, s.s3, s.r3, w_sem,
+        s.qs, s.kvrow, s.sc, s.p, s.ot, s.inv, s.slots, s.att, s.g, s.acc, s.q, s.weight, s.kv, s.table, s.og,
+        s.ls, s.lo, s.s1, s.r1, s.s2, s.r2, s.s3, s.r3, w_sem, q_sem,
         s.og_send, s.og_recv, s.kv_send, s.kv_recv, s.lo_send, s.lo_recv,
         s.send1, s.recv1, s.send2, s.recv2, s.send3, s.recv3, s.send4, s.recv4, s.send5, s.recv5,
     ) = refs
@@ -254,6 +253,8 @@
     me = Place()
     w_copy = pltpu.make_async_copy(weight, s.weight, w_sem)
     w_copy.start()
+    q_copy = pltpu.make_async_copy(query, s.q, q_sem)
+    q_copy.start()
     mine = pl.multiple_of(me.c * ROWS, ROWS)
     s.kv[pl.ds(mine, ROWS), :, :HD] = key[...]
     s.kv[pl.ds(mine, ROWS), :, HD:] = value[...]
@@ -363,6 +364,7 @@
     og_across(0)
     og_near(2)
     w_copy.wait()
+    q_copy.wait()
     for owner in (me.h, me.xm, me.xp):
         project_early(owner, owner is me.h)
     kv_ready(0)
@@ -444,9 +446,9 @@
     def lo_final(k):
         layer_out[pl.ds(k * OG_ROWS, OG_ROWS)] = lo_add(me.h, k, (3, 4, 6))
 
-    forward_row(0, 2, index, q, s)
+    forward_row(0, 2, index, s.q, s)
     kv_near(2)
-    forward_row(1, 4, index, q, s)
+    forward_row(1, 4, index, s.q, s)
     og_far(3)
     kv_far(1)
     og_near(1)
@@ -471,7 +473,7 @@
             def _():
                 og_far(KV_PARTS - 1 - k)
 
-            forward_row(2 * k + half, NCH, index, q, s)
+            forward_row(2 * k + half, NCH, index, s.q, s)
 
         shares(k)
 
@@ -672,7 +674,7 @@
     return pl.pallas_call(
         functools.partial(layer_kernel, n_ctx),
         out_shape=[jax.ShapeDtypeStruct(shape, low) for shape in (wide, wide, narrow, narrow)],
-        in_specs=[smem] + [vmem] * 4 + [pl.BlockSpec(memory_space=pl.ANY)],
+        in_specs=[smem, pl.BlockSpec(memory_space=pl.ANY)] + [vmem] * 3 + [pl.BlockSpec(memory_space=pl.ANY)],
         out_specs=[vmem] * 4,
         scratch_shapes=[
             pltpu.VMEM((ROWS, QN, HD), low),
@@ -681,10 +683,11 @@
             pltpu.VMEM((CHUNKS, CK, QN), low),
             pltpu.VMEM((ROWS, HD, QN), low),
             pltpu.VMEM((ROWS, 8, QN), jnp.float32),
-            pltpu.VMEM((NOSLOT + 1, BLK, 2 * HD), low),
+            pltpu.VMEM((FIRST + CHUNKS * EPC, BLK, 2 * HD), low),
             pltpu.VMEM(wide, low),
             pltpu.VMEM(wide, low),
             pltpu.VMEM(wide, jnp.float32),
+            pltpu.VMEM(wide, low),
             pltpu.VMEM(weight.shape, low),
             pltpu.VMEM((n_ctx * ROWS, BLK, 2 * HD), low),
             pltpu.VMEM((n_ctx * ROWS, BLK, 2 * HD), low),
@@ -697,6 +700,7 @@
             pltpu.VMEM((ROWS, 3, 2, BLK, 2 * HD), low),
             pltpu.VMEM((ROWS, BLK, 2 * HD), low),
             pltpu.VMEM((ROWS, BLK, 2 * HD), low),
+            sem,
             sem,
             sem((7, OG_PARTS)), sem((7, OG_PARTS)),
             sem((15, KV_PARTS)), sem((15, KV_PARTS)),

time: 89.3 us -> 89.2 us (level)
  no operation moved by 1% of the time
where the time goes in v4:
time: 89.2 us; the launch traced here: 89 us
  Pallas kernels  85.5 us (96%)
  other arithmetic  2.78 us (3%)
    pallas_call x1, Pallas kernels, layer(): pl.pallas_call(functools.partial(layer_kernel, n_ctx), out_shape=[jax.Sha...  83.2 us
    pallas_call x1, Pallas kernels, hand_over(): pl.pallas_call(hand_over_kernel, out_shape=[jax.ShapeDtypeStruct(x.shape,...  2.34 us

profile of v4, /device:TPU:2, one launch (start us, length us, event | category | flops | bytes accessed | tf_op | source)
XLA Modules:
  0.0 89.0 jit_solution(11715608841384751803)
XLA Ops:
  0.7 0.8 broadcast_subtract_fusion
  1.4 0.8 fusion.10
  2.2 0.2 convert_reduce_fusion
  2.4 0.1 broadcast_add_fusion
  2.5 0.9 %select_reduce_fusion.index = s32[8,169]{1,0:T(8,128)} fusion(s32[8,40]{1,0:T(8,128)S(1)} %get-tuple-element.33, s32[8,40]{1,0:T(8,128)S(1)} %get-tuple-element.32, s32[8,40]{1,0:T(8,128)S(1)} %get-tuple-element.31, s32[169]{0:T(256)S(1)} %iota_add_fusion, s32[8,40]{1,0:T(8,128)S(1)} %get-tuple-element.30, s32[8,40]{1,0:T(8,128)S(1)} %get-tuple-element.28, ...), kind=kLoop, calls=%fused_computation | loop fusion | flops 431288 | bytes 13142 | tf_op jit(solution)/shard_map/reduce_sum | solution.py:50
  3.4 83.2 %layer.1 = (bf16[8,64,512]{2,1,0:T(8,128)(2,1)}, bf16[8,64,512]{2,1,0:T(8,128)(2,1)}, bf16[8,64,128]{2,1,0:T(8,128)(2,1)}, bf16[8,64,128]{2,1,0:T(8,128)(2,1)}) custom-call(s32[8,169]{1,0:T(8,128)} %select_reduce_fusion.index, bf16[8,64,512]{2,1,0:T(8,128)(2,1)} %bitcast.18, bf16[8,64,128]{2,1,0:T(8,128)(2,1)} %bitcast.20, bf16[8,64,128]{2,1,0:T(8,128)(2,1)} %bitcast.21, ...), custom_call_target="tpu_custom_call" | custom-call | tf_op jit(solution)/shard_map/layer/pallas_call | solution.py:674
  86.6 2.3 %hand_over.1 = (bf16[8,64,512]{2,1,0:T(8,128)(2,1)}, bf16[8,64,512]{2,1,0:T(8,128)(2,1)}, bf16[8,64,128]{2,1,0:T(8,128)(2,1)}, bf16[8,64,128]{2,1,0:T(8,128)(2,1)}) custom-call(bf16[8,64,512]{2,1,0:T(8,128)(2,1)} %get-tuple-element.12.refs_0_, bf16[8,64,512]{2,1,0:T(8,128)(2,1)} %get-tuple-element.13.refs_1_, bf16[8,64,128]{2,1,0:T(8,128)(2,1)} %get-tuple-element.14.refs_2_, ...), custom_call_target="tpu_custom_call" | custom-call | tf_op jit(solution)/shard_map/hand_over/pallas_call | solution.py:659
  (5 shorter events, 0.0 us)
